TPU v7x, 512 devices: a whole 4x8x8 slice. The times are simulated.
512 devices in a mesh: dp: 32 (over x_hi, y, core), seq: 16 (over x_lo, z).
Axes of the slice: x: 4 (x_hi: 2, x_lo: 2; x = x_hi * 2 + x_lo), y: 8, z: 8, core: 2. Of those that a mesh axis runs over, the one named last changes fastest.
Arguments:
- query: bfloat16 [32, 2048, 4096], P('dp', 'seq'), may hold values from -108 to 108
- keys: bfloat16 [32, 2048, 512], P('dp', 'seq'), may hold values from -9 to 9
- values: bfloat16 [32, 2048, 512], P('dp', 'seq'), may hold values from -6 to 6
- grad_out: bfloat16 [32, 2048, 4096], P('dp', 'seq'), may hold values from -6 to 6
- positions: int32 [32, 2048], P('dp', 'seq'), may hold values from 0 to 16383, as said below
- q_scale: float32 [4096], replicated, may hold values from 0.1 to 1.9
- k_scale: float32 [512], replicated, may hold values from 0.1 to 1.9
Outputs:
- grad_query: bfloat16 [32, 2048, 4096], P('dp', 'seq')
- grad_keys: bfloat16 [32, 2048, 512], P('dp', 'seq')
- grad_values: bfloat16 [32, 2048, 512], P('dp', 'seq')
- grad_qscale: float32 [4096], replicated
- grad_kscale: float32 [512], replicated
Inputs may be any that keep to these rules, and one draw needn't show every extreme that they name: Along each sequence positions rise by 1 or 2 from one token to the next; some sequence ends at position 16383.
All inputs are finite; a program needn't handle non-finite values.
Results may differ from a plain program's by a relative error of at most 0.035.
Values may be sent and summed in bfloat16 or wider, within the bound.
No kernel may reach another device: no remote copies, remote signals or barrier semaphores. Data moves between devices by JAX's collectives and lax.ppermute only.
A program may use at most 128 MiB of HBM per device.

v0:
```python
import math

import jax
import jax.numpy as jnp
from jax import lax
from jax.sharding import PartitionSpec as P

HQ = 32
HK = 4
HD = 128


rope_base = 1000000.0


def angles(pos, width):
    half = width // 2
    freq = rope_base ** (-(jnp.arange(half, dtype=jnp.float32) * 2.0) / width)
    angle = pos.astype(jnp.float32)[..., None] * freq
    return (jnp.cos(angle)[..., None, :], jnp.sin(angle)[..., None, :])


def rotate(inputs, pos):
    half = inputs.shape[-1] // 2
    cosine, sine = angles(pos, inputs.shape[-1])
    first = inputs[..., :half]
    second = inputs[..., half:]
    return jnp.concatenate(
        [first * cosine - second * sine, second * cosine + first * sine], axis=-1
    )


def unrotate(grads, pos):
    half = grads.shape[-1] // 2
    cosine, sine = angles(pos, grads.shape[-1])
    first = grads[..., :half]
    second = grads[..., half:]
    return jnp.concatenate(
        [first * cosine + second * sine, second * cosine - first * sine], axis=-1
    )


def attend_backward(q_heads, d_heads, key_col, val_col):
    seq_here, length, per_dev, width = q_heads.shape
    block = math.gcd(length, min(length, max(1, 512 // (per_dev * seq_here))))
    factor = 1.0 / math.sqrt(width)
    grad_k = jnp.zeros((seq_here, length, per_dev, width), jnp.float32)
    grad_v = jnp.zeros((seq_here, length, per_dev, width), jnp.float32)
    pieces = []
    for start in range(0, length, block):
        end = start + block
        q_blk = q_heads[:, start:end]
        d_blk = d_heads[:, start:end]
        k_blk = key_col[:, :end]
        v_blk = val_col[:, :end]
        scores = (
            jnp.einsum("sqhd,skd->shqk", q_blk, k_blk, preferred_element_type=jnp.float32) * factor
        )
        rows = start + jnp.arange(block)[:, None]
        cols = jnp.arange(end)[None, :]
        scores = jnp.where((cols <= rows)[None, None], scores, -jnp.inf)
        top = jnp.max(scores, axis=-1, keepdims=True)
        weights = jnp.exp(scores - top)
        probs = weights / jnp.sum(weights, axis=-1, keepdims=True)
        probs_b = probs.astype(jnp.bfloat16)
        attended = jnp.einsum("shqk,skd->sqhd", probs_b, v_blk, preferred_element_type=jnp.float32)
        delta = jnp.sum(d_blk.astype(jnp.float32) * attended, axis=-1)
        dprob = jnp.einsum("sqhd,skd->shqk", d_blk, v_blk, preferred_element_type=jnp.float32)
        dscore = (probs * (dprob - jnp.transpose(delta, (0, 2, 1))[..., None]) * factor).astype(
            jnp.bfloat16
        )
        pieces.append(
            jnp.einsum("shqk,skd->sqhd", dscore, k_blk, preferred_element_type=jnp.float32).astype(
                jnp.bfloat16
            )
        )
        grad_k = grad_k.at[:, :end].add(
            jnp.einsum("shqk,sqhd->skhd", dscore, q_blk, preferred_element_type=jnp.float32)
        )
        grad_v = grad_v.at[:, :end].add(
            jnp.einsum("shqk,sqhd->skhd", probs_b, d_blk, preferred_element_type=jnp.float32)
        )
    return (jnp.concatenate(pieces, axis=1), grad_k, grad_v)


def shards(query, keys, values, grad_out, positions, q_scale, k_scale):
    seq_here = query.shape[0]
    tokens_here = query.shape[1]
    group = HQ // HK
    q_gain = q_scale.reshape(HQ, HD)
    k_gain = k_scale.reshape(HK, HD)
    q_raw = query.reshape(seq_here, tokens_here, HQ, HD)
    k_raw = keys.reshape(seq_here, tokens_here, HK, HD)
    q_rot = rotate(q_raw.astype(jnp.float32) * q_gain, positions).astype(jnp.bfloat16)
    k_rot = rotate(k_raw.astype(jnp.float32) * k_gain, positions).astype(jnp.bfloat16)
    v_tok = values.reshape(seq_here, tokens_here, HK, HD)
    d_tok = grad_out.reshape(seq_here, tokens_here, HQ, HD)
    q_heads, d_heads = (
        lax.all_to_all(q_rot, "seq", split_axis=2, concat_axis=1, tiled=True),
        lax.all_to_all(d_tok, "seq", split_axis=2, concat_axis=1, tiled=True),
    )
    k_heads, v_heads = (
        lax.all_to_all(
            jnp.repeat(k_rot, group, axis=2), "seq", split_axis=2, concat_axis=1, tiled=True
        ),
        lax.all_to_all(
            jnp.repeat(v_tok, group, axis=2), "seq", split_axis=2, concat_axis=1, tiled=True
        ),
    )
    dq_heads, grad_k, grad_v = attend_backward(
        q_heads, d_heads, k_heads[:, :, 0, :], v_heads[:, :, 0, :]
    )
    dq_tok = lax.all_to_all(dq_heads, "seq", split_axis=1, concat_axis=2, tiled=True)
    dk_tok, dv_tok = (
        lax.all_to_all(grad_k, "seq", split_axis=1, concat_axis=2, tiled=True),
        lax.all_to_all(grad_v, "seq", split_axis=1, concat_axis=2, tiled=True),
    )
    dk_sum = dk_tok.reshape(seq_here, tokens_here, HK, group, HD).sum(axis=3)
    dv_sum = dv_tok.reshape(seq_here, tokens_here, HK, group, HD).sum(axis=3)
    dk_rot = lax.optimization_barrier(dk_sum.astype(jnp.bfloat16)).astype(jnp.float32)
    back_q = unrotate(dq_tok.astype(jnp.float32), positions)
    back_k = unrotate(dk_rot, positions)
    grad_query = (back_q * q_gain).astype(jnp.bfloat16).reshape(seq_here, tokens_here, HQ * HD)
    grad_keys = (back_k * k_gain).astype(jnp.bfloat16).reshape(seq_here, tokens_here, HK * HD)
    grad_values = dv_sum.astype(jnp.bfloat16).reshape(seq_here, tokens_here, HK * HD)
    term_q = jnp.sum(q_raw.astype(jnp.float32) * back_q, axis=(0, 1)).reshape(HQ * HD)
    term_k = jnp.sum(k_raw.astype(jnp.float32) * back_k, axis=(0, 1)).reshape(HK * HD)
    total_q, total_k = lax.psum((term_q, term_k), ("dp", "seq"))
    return (grad_query, grad_keys, grad_values, total_q, total_k)


def solution(mesh):
    return jax.shard_map(
        shards,
        mesh=mesh,
        in_specs=(
            P("dp", "seq", None),
            P("dp", "seq", None),
            P("dp", "seq", None),
            P("dp", "seq", None),
            P("dp", "seq"),
            P(),
            P(),
        ),
        out_specs=(P("dp", "seq", None), P("dp", "seq", None), P("dp", "seq", None), P(), P()),
        check_vma=False,
    )
```

profile of v0, /device:TPU:1, one launch (start us, length us, event | category | flops | bytes accessed | tf_op | source)
XLA Modules:
  0.0 431.1 jit_solution(4026135346759510768)
XLA Ops:
  5.2 11.9 %all-to-all-start = ((bf16[1,128,32,128]{3,1,0,2:T(8,128)(2,1)}), bf16[1,128,32,128]{3,1,0,2:T(8,128)(2,1)S(1)}, u32[]{:S(2)}, u32[]{:S(2)}) async-start(bf16[1,128,32,128]{3,1,0,2:T(8,128)(2,1)} %bitcast.5), calls=%async_computation | async-start | bytes 2097152 | tf_op jit(solution)/shard_map/all_to_all | solution.py:103
  17.2 25.6 %all-to-all-done = bf16[1,128,32,128]{3,1,0,2:T(8,128)(2,1)S(1)} async-done(((bf16[1,128,32,128]{3,1,0,2:T(8,128)(2,1)}), bf16[1,128,32,128]{3,1,0,2:T(8,128)(2,1)S(1)}, u32[]{:S(2)}, u32[]{:S(2)}) %all-to-all-start) | async-done | bytes 1048608 | tf_op jit(solution)/shard_map/all_to_all | solution.py:103
  44.1 6.2 %all-to-all-start.2 = ((bf16[1,128,32,128]{3,1,0,2:T(8,128)(2,1)}), bf16[1,128,32,128]{3,1,0,2:T(8,128)(2,1)}, u32[]{:S(2)}, u32[]{:S(2)}) async-start(bf16[1,128,32,128]{3,1,0,2:T(8,128)(2,1)} %bitcast.22), calls=%async_computation.2 | async-start | bytes 2097152 | tf_op jit(solution)/shard_map/all_to_all | solution.py:106
  55.8 20.0 %all-to-all-done.2 = bf16[1,128,32,128]{3,1,0,2:T(8,128)(2,1)} async-done(((bf16[1,128,32,128]{3,1,0,2:T(8,128)(2,1)}), bf16[1,128,32,128]{3,1,0,2:T(8,128)(2,1)}, u32[]{:S(2)}, u32[]{:S(2)}) %all-to-all-start.2) | async-done | bytes 1048608 | tf_op jit(solution)/shard_map/all_to_all | solution.py:106
  75.8 6.2 %all-to-all-start.3 = ((bf16[1,128,32,128]{1,3,0,2:T(8,128)(2,1)}), bf16[1,128,32,128]{1,3,0,2:T(8,128)(2,1)}, u32[]{:S(2)}, u32[]{:S(2)}) async-start(bf16[1,128,32,128]{1,3,0,2:T(8,128)(2,1)} %bitcast.1072), calls=%async_computation.3 | async-start | bytes 2097152 | tf_op jit(solution)/shard_map/all_to_all | solution.py:100
  87.2 20.4 %all-to-all-done.3 = bf16[1,128,32,128]{1,3,0,2:T(8,128)(2,1)} async-done(((bf16[1,128,32,128]{1,3,0,2:T(8,128)(2,1)}), bf16[1,128,32,128]{1,3,0,2:T(8,128)(2,1)}, u32[]{:S(2)}, u32[]{:S(2)}) %all-to-all-start.3) | async-done | bytes 1048608 | tf_op jit(solution)/shard_map/all_to_all | solution.py:100
  107.5 6.2 %all-to-all-start.1 = ((bf16[1,128,32,128]{1,3,0,2:T(8,128)(2,1)}), bf16[1,128,32,128]{1,3,0,2:T(8,128)(2,1)S(1)}, u32[]{:S(2)}, u32[]{:S(2)}) async-start(bf16[1,128,32,128]{1,3,0,2:T(8,128)(2,1)} %maximum_bitcast_fusion), calls=%async_computation.1 | async-start | bytes 2097152 | tf_op jit(solution)/shard_map/all_to_all | solution.py:99
  117.0 2.3 copy.610
  119.3 2.3 copy.613
  123.5 15.7 %all-to-all-done.1 = bf16[1,128,32,128]{1,3,0,2:T(8,128)(2,1)S(1)} async-done(((bf16[1,128,32,128]{1,3,0,2:T(8,128)(2,1)}), bf16[1,128,32,128]{1,3,0,2:T(8,128)(2,1)S(1)}, u32[]{:S(2)}, u32[]{:S(2)}) %all-to-all-start.1) | async-done | bytes 1048608 | tf_op jit(solution)/shard_map/all_to_all | solution.py:99
  177.1 3.6 copy.655
  180.8 6.6 %all-to-all-start.4 = ((bf16[1,2048,2,128]{3,2,0,1:T(2,128)(2,1)}), bf16[1,2048,2,128]{3,2,0,1:T(2,128)(2,1)}, u32[]{:S(2)}, u32[]{:S(2)}) async-start(bf16[1,2048,2,128]{3,2,0,1:T(2,128)(2,1)} %copy.655), calls=%async_computation.4 | async-start | bytes 2097152 | tf_op jit(solution)/shard_map/all_to_all | solution.py:113
  195.7 8.6 %copy.679 = f32[1,2048,2,128]{3,2,0,1:T(2,128)} copy(f32[1,2048,2,128]{3,1,2,0:T(8,128)S(1)} %fusion.41) | data formatting | bytes 4194304 | tf_op jit(solution)/shard_map/add | solution.py:80
  204.3 8.6 %all-to-all-done.4 = bf16[1,2048,2,128]{3,2,0,1:T(2,128)(2,1)} async-done(((bf16[1,2048,2,128]{3,2,0,1:T(2,128)(2,1)}), bf16[1,2048,2,128]{3,2,0,1:T(2,128)(2,1)}, u32[]{:S(2)}, u32[]{:S(2)}) %all-to-all-start.4) | async-done | bytes 1048608 | tf_op jit(solution)/shard_map/all_to_all | solution.py:113
  212.9 6.2 %all-to-all-start.6 = ((f32[1,2048,2,128]{3,2,0,1:T(2,128)}), f32[1,2048,2,128]{3,2,0,1:T(2,128)}, u32[]{:S(2)}, u32[]{:S(2)}) async-start(f32[1,2048,2,128]{3,2,0,1:T(2,128)} %copy.679), calls=%async_computation.6 | async-start | bytes 4194304 | tf_op jit(solution)/shard_map/all_to_all | solution.py:116
  228.1 2.4 copy.676
  230.4 36.6 %all-to-all-done.6 = f32[1,2048,2,128]{3,2,0,1:T(2,128)} async-done(((f32[1,2048,2,128]{3,2,0,1:T(2,128)}), f32[1,2048,2,128]{3,2,0,1:T(2,128)}, u32[]{:S(2)}, u32[]{:S(2)}) %all-to-all-start.6) | async-done | bytes 2097184 | tf_op jit(solution)/shard_map/all_to_all | solution.py:116
  267.0 7.2 %all-to-all-start.5 = ((f32[1,2048,2,128]{3,2,0,1:T(2,128)}), f32[1,2048,2,128]{3,2,0,1:T(2,128)S(1)}, u32[]{:S(2)}, u32[]{:S(2)}) async-start(f32[1,2048,2,128]{3,2,0,1:T(2,128)} %copy.676), calls=%async_computation.5 | async-start | bytes 4194304 | tf_op jit(solution)/shard_map/all_to_all | solution.py:115
  276.0 2.7 fusion.220
  280.9 3.2 copy.757
  289.6 8.8 %reduce_sum.247 = f32[2048,128]{1,0:T(8,128)S(1)} reduce(f32[1,2048,2,128]{3,2,0,1:T(2,128)} %all-to-all-done.6, f32[]{:T(128)} %constant.395.clone.1), dimensions={0,2}, to_apply=%region_26.27 | reduce | flops 262144 | bytes 3145732 | tf_op jit(solution)/shard_map/reduce_sum | solution.py:119
  299.5 22.5 %all-to-all-done.5 = f32[1,2048,2,128]{3,2,0,1:T(2,128)S(1)} async-done(((f32[1,2048,2,128]{3,2,0,1:T(2,128)}), f32[1,2048,2,128]{3,2,0,1:T(2,128)S(1)}, u32[]{:S(2)}, u32[]{:S(2)}) %all-to-all-start.5) | async-done | bytes 2097184 | tf_op jit(solution)/shard_map/all_to_all | solution.py:115
  321.9 7.8 %reduce_sum.242 = f32[2048,128]{1,0:T(8,128)S(1)} reduce(f32[1,2048,2,128]{3,2,0,1:T(2,128)S(1)} %all-to-all-done.5, f32[]{:T(128)} %constant.395.clone.1), dimensions={0,2}, to_apply=%region_24.25 | reduce | flops 262144 | bytes 3145732 | tf_op jit(solution)/shard_map/reduce_sum | solution.py:118
  332.3 98.6 %all-reduce.2 = (f32[4096]{0:T(1024)}, f32[512]{0:T(512)}) all-reduce(f32[4096]{0:T(1024)S(1)} %get-tuple-element.254, f32[512]{0:T(512)S(1)} %get-tuple-element.262), channel_id=1, replica_groups=mesh['dp'=32,'seq'=16] {'dp','seq'}, use_global_device_ids=true, to_apply=%region_29.30 | all-reduce | flops 4608 | bytes 36864 | tf_op jit(solution)/shard_map/psum | solution.py:128
  (245 shorter events, 89.1 us)
Async XLA Ops:
  3.3 78.7 %copy-start.40 = (f32[128,64]{0,1:T(8,128)}, f32[128,64]{0,1:T(8,128)S(1)}, u32[]{:S(2)}) copy-start(f32[128,64]{0,1:T(8,128)S(1)} %get-tuple-element.264) | copy-start | bytes 98308
  3.4 78.7 %copy-start.42 = (f32[128,64]{0,1:T(8,128)}, f32[128,64]{0,1:T(8,128)S(1)}, u32[]{:S(2)}) copy-start(f32[128,64]{0,1:T(8,128)S(1)} %get-tuple-element.265) | copy-start | bytes 98308
  3.6 13.5 %copy-start.51 = (bf16[1,128,512]{2,1,0:T(8,128)(2,1)S(1)}, bf16[1,128,512]{2,1,0:T(8,128)(2,1)}, u32[]{:S(2)}) copy-start(bf16[1,128,512]{2,1,0:T(8,128)(2,1)} %param.45) | copy-start | bytes 393220
  5.2 37.6 %all-to-all-start = ((bf16[1,128,32,128]{3,1,0,2:T(8,128)(2,1)}), bf16[1,128,32,128]{3,1,0,2:T(8,128)(2,1)S(1)}, u32[]{:S(2)}, u32[]{:S(2)}) async-start(bf16[1,128,32,128]{3,1,0,2:T(8,128)(2,1)} %bitcast.5), calls=%async_computation | async-start | bytes 2097152 | tf_op jit(solution)/shard_map/all_to_all | solution.py:103
  17.1 33.2 %copy-start.38 = (bf16[1,128,4096]{2,1,0:T(8,128)(2,1)S(1)}, bf16[1,128,4096]{2,1,0:T(8,128)(2,1)}, u32[]{:S(2)}) copy-start(bf16[1,128,4096]{2,1,0:T(8,128)(2,1)} %param.43) | copy-start | bytes 3145732
  44.1 6.9 %copy-start.39 = (bf16[1,128,4096]{2,1,0:T(8,128)(2,1)S(1)}, bf16[1,128,4096]{2,1,0:T(8,128)(2,1)}, u32[]{:S(2)}) copy-start(bf16[1,128,4096]{2,1,0:T(8,128)(2,1)} %param.46) | copy-start | bytes 3145732
  44.1 31.7 %all-to-all-start.2 = ((bf16[1,128,32,128]{3,1,0,2:T(8,128)(2,1)}), bf16[1,128,32,128]{3,1,0,2:T(8,128)(2,1)}, u32[]{:S(2)}, u32[]{:S(2)}) async-start(bf16[1,128,32,128]{3,1,0,2:T(8,128)(2,1)} %bitcast.22), calls=%async_computation.2 | async-start | bytes 2097152 | tf_op jit(solution)/shard_map/all_to_all | solution.py:106
  75.8 31.8 %all-to-all-start.3 = ((bf16[1,128,32,128]{1,3,0,2:T(8,128)(2,1)}), bf16[1,128,32,128]{1,3,0,2:T(8,128)(2,1)}, u32[]{:S(2)}, u32[]{:S(2)}) async-start(bf16[1,128,32,128]{1,3,0,2:T(8,128)(2,1)} %bitcast.1072), calls=%async_computation.3 | async-start | bytes 2097152 | tf_op jit(solution)/shard_map/all_to_all | solution.py:100
  83.4 30.3 %copy-start.55 = (s32[256]{0:T(256)S(1)}, s32[256]{0:T(256)}, u32[]{:S(2)}) copy-start(s32[256]{0:T(256)} %iota_add_fusion.1) | copy-start | bytes 3076
  84.2 31.8 %copy-start.28 = (bf16[1,128,32,128]{3,1,0,2:T(8,128)(2,1)S(1)}, bf16[1,128,32,128]{3,1,0,2:T(8,128)(2,1)}, u32[]{:S(2)}) copy-start(bf16[1,128,32,128]{3,1,0,2:T(8,128)(2,1)} %copy-done.27) | copy-start | bytes 3145732
  107.5 31.7 %all-to-all-start.1 = ((bf16[1,128,32,128]{1,3,0,2:T(8,128)(2,1)}), bf16[1,128,32,128]{1,3,0,2:T(8,128)(2,1)S(1)}, u32[]{:S(2)}, u32[]{:S(2)}) async-start(bf16[1,128,32,128]{1,3,0,2:T(8,128)(2,1)} %maximum_bitcast_fusion), calls=%async_computation.1 | async-start | bytes 2097152 | tf_op jit(solution)/shard_map/all_to_all | solution.py:99
  123.1 27.8 %copy-start.24 = (bf16[1,16,128,2,128]{4,2,1,3,0:T(8,128)(2,1)}, bf16[1,16,128,2,128]{4,2,1,3,0:T(8,128)(2,1)S(1)}, u32[]{:S(2)}) copy-start(bf16[1,16,128,2,128]{4,2,1,3,0:T(8,128)(2,1)S(1)} %copy.614) | copy-start | bytes 3145732
  123.5 23.0 %copy-start.45 = (bf16[1,2048,128]{2,1,0:T(8,128)(2,1)}, bf16[1,2048,128]{2,1,0:T(8,128)(2,1)S(1)}, u32[]{:S(2)}) copy-start(bf16[1,2048,128]{2,1,0:T(8,128)(2,1)S(1)} %slice_bitcast_fusion.6) | copy-start | bytes 1572868
  142.0 22.8 %copy-start.22 = (bf16[1,16,128,2,128]{4,2,1,3,0:T(8,128)(2,1)}, bf16[1,16,128,2,128]{4,2,1,3,0:T(8,128)(2,1)S(1)}, u32[]{:S(2)}) copy-start(bf16[1,16,128,2,128]{4,2,1,3,0:T(8,128)(2,1)S(1)} %copy.608) | copy-start | bytes 3145732
  145.6 24.0 %copy-start.34 = (bf16[2,256,512]{1,2,0:T(8,128)(2,1)}, bf16[2,256,512]{1,2,0:T(8,128)(2,1)S(1)}, u32[]{:S(2)}) copy-start(bf16[2,256,512]{1,2,0:T(8,128)(2,1)S(1)} %fusion.84) | copy-start | bytes 1572868
  151.6 20.2 %copy-start.18 = (bf16[2,256,1024]{1,2,0:T(8,128)(2,1)}, bf16[2,256,1024]{1,2,0:T(8,128)(2,1)S(1)}, u32[]{:S(2)}) copy-start(bf16[2,256,1024]{1,2,0:T(8,128)(2,1)S(1)} %fusion.65) | copy-start | bytes 3145732
  156.9 15.9 %copy-start.14 = (bf16[2,256,1280]{1,2,0:T(8,128)(2,1)}, bf16[2,256,1280]{1,2,0:T(8,128)(2,1)S(1)}, u32[]{:S(2)}) copy-start(bf16[2,256,1280]{1,2,0:T(8,128)(2,1)S(1)} %fusion.28) | copy-start | bytes 3932164
  160.6 13.2 %copy-start.10 = (bf16[2,256,1536]{1,2,0:T(8,128)(2,1)}, bf16[2,256,1536]{1,2,0:T(8,128)(2,1)S(1)}, u32[]{:S(2)}) copy-start(bf16[2,256,1536]{1,2,0:T(8,128)(2,1)S(1)} %fusion.29) | copy-start | bytes 4718596
  165.1 9.7 %copy-start.6 = (bf16[2,256,1792]{1,2,0:T(8,128)(2,1)}, bf16[2,256,1792]{1,2,0:T(8,128)(2,1)S(1)}, u32[]{:S(2)}) copy-start(bf16[2,256,1792]{1,2,0:T(8,128)(2,1)S(1)} %fusion.30) | copy-start | bytes 5505028
  180.8 32.2 %all-to-all-start.4 = ((bf16[1,2048,2,128]{3,2,0,1:T(2,128)(2,1)}), bf16[1,2048,2,128]{3,2,0,1:T(2,128)(2,1)}, u32[]{:S(2)}, u32[]{:S(2)}) async-start(bf16[1,2048,2,128]{3,2,0,1:T(2,128)(2,1)} %copy.655), calls=%async_computation.4 | async-start | bytes 2097152 | tf_op jit(solution)/shard_map/all_to_all | solution.py:113
  204.3 14.8 %copy-start.23 = (bf16[1,16,128,2,128]{4,2,1,3,0:T(8,128)(2,1)S(1)}, bf16[1,16,128,2,128]{4,2,1,3,0:T(8,128)(2,1)}, u32[]{:S(2)}) copy-start(bf16[1,16,128,2,128]{4,2,1,3,0:T(8,128)(2,1)} %copy-done.22) | copy-start | bytes 3145732
  204.3 14.8 %copy-start.37 = (bf16[2,256,256]{1,2,0:T(8,128)(2,1)S(1)}, bf16[2,256,256]{1,2,0:T(8,128)(2,1)}, u32[]{:S(2)}) copy-start(bf16[2,256,256]{1,2,0:T(8,128)(2,1)} %copy-done.36) | copy-start | bytes 786436
  212.9 54.1 %all-to-all-start.6 = ((f32[1,2048,2,128]{3,2,0,1:T(2,128)}), f32[1,2048,2,128]{3,2,0,1:T(2,128)}, u32[]{:S(2)}, u32[]{:S(2)}) async-start(f32[1,2048,2,128]{3,2,0,1:T(2,128)} %copy.679), calls=%async_computation.6 | async-start | bytes 4194304 | tf_op jit(solution)/shard_map/all_to_all | solution.py:116
  267.0 55.0 %all-to-all-start.5 = ((f32[1,2048,2,128]{3,2,0,1:T(2,128)}), f32[1,2048,2,128]{3,2,0,1:T(2,128)S(1)}, u32[]{:S(2)}, u32[]{:S(2)}) async-start(f32[1,2048,2,128]{3,2,0,1:T(2,128)} %copy.676), calls=%async_computation.5 | async-start | bytes 4194304 | tf_op jit(solution)/shard_map/all_to_all | solution.py:115
  (43 other events, 81.5 us)
where the time goes:
time: 438 us; the launch traced here: 431 us
  waiting for transfers between devices  149 us (34%)
  blocking collectives  98.6 us (23%)
  local copies, waits for them, and re-layouts  58.5 us (13%)
  starting transfers between devices  50.5 us (12%)
  other arithmetic  38.9 us (9%)
  matrix products  33.4 us (8%)
    psum x1, blocking collectives, shards(): total_q, total_k = lax.psum((term_q, term_k), ('dp', 'seq'))  98.6 us
    all_to_all x1, waiting for transfers between devices, shards(): lax.all_to_all(grad_v, 'seq', split_axis=1, concat_axis=2, tiled=True)  36.6 us
    all_to_all x1, waiting for transfers between devices, shards(): lax.all_to_all(jnp.repeat(k_rot, group, axis=2), 'seq', split_axis=2, con...  25.6 us
    unnamed x128, local copies, waits for them, and re-layouts  25.1 us
    all_to_all x1, waiting for transfers between devices, shards(): lax.all_to_all(grad_k, 'seq', split_axis=1, concat_axis=2, tiled=True)  22.5 us
    all_to_all x1, waiting for transfers between devices, shards(): lax.all_to_all(d_tok, 'seq', split_axis=2, concat_axis=1, tiled=True)  20.4 us
    all_to_all x1, waiting for transfers between devices, shards(): lax.all_to_all(jnp.repeat(v_tok, group, axis=2), 'seq', split_axis=2, con...  20 us
    all_to_all x1, waiting for transfers between devices, shards(): lax.all_to_all(q_rot, 'seq', split_axis=2, concat_axis=1, tiled=True)  15.7 us
  transfers between devices with their start and end apart: 7, of which 7 were waited for; matrix products, arithmetic and copies ran while one was open for 15% of the time, Pallas kernels for 0%

commit v1 on v0

v1 whole, which is shorter than its diff:
```python
import math

import jax
import jax.numpy as jnp
from jax import lax
from jax.experimental import pallas as pl
from jax.experimental.pallas import tpu as pltpu
from jax.sharding import PartitionSpec as P

HQ = 32
HK = 4
HD = 128
BLK = 128
EXTRA = 16
SUB = 4
ROWS = 2 * SUB * BLK
CHUNK = 256
KEYS = 512
FACTOR = 1.0 / math.sqrt(HD)
EXP2 = FACTOR * math.log2(math.e)
NEG = -1e30
rope_base = 1000000.0

f32 = jnp.float32
bf16 = jnp.bfloat16
VMEM = pl.BlockSpec(memory_space=pltpu.VMEM)
SMEM = pl.BlockSpec(memory_space=pltpu.SMEM)
ANY = pl.BlockSpec(memory_space=pl.ANY)


def shape(dims, dtype):
    return jax.ShapeDtypeStruct(dims, dtype)


def params(mib):
    return pltpu.CompilerParams(vmem_limit_bytes=mib << 20)


def turn(x, c, s):
    return x * c + pltpu.roll(x, HD // 2, 1) * s


def unturn(x, c, s):
    return x * c - pltpu.roll(x, HD // 2, 1) * s


def two_parts(x):
    high = lax.reduce_precision(x, 8, 7)
    return jnp.concatenate([high, x - high], axis=-1).astype(bf16)


def angle_tables():
    half = HD // 2
    freq = rope_base ** (-(jnp.arange(half, dtype=f32) * 2.0) / HD)
    freq = jnp.concatenate([freq, freq])[None]
    steps = jnp.arange(BLK, dtype=f32)[:, None]
    out = []
    for angle in (steps * BLK * freq, steps * freq):
        out.append(two_parts(jnp.concatenate([jnp.cos(angle), jnp.sin(angle)], axis=-1)))
    return jnp.stack(out)


def full_table(pos):
    half = HD // 2
    freq = rope_base ** (-(jnp.arange(half, dtype=f32) * 2.0) / HD)
    angle = pos.astype(f32)[:, None] * freq
    cosine, sine = jnp.cos(angle), jnp.sin(angle)
    return jnp.concatenate([cosine, cosine, -sine, sine], axis=-1)


def pack_kernel(place_ref, q_ref, d_ref, k_ref, v_ref, pos_ref, *outs):
    own_ref, x_ref, za_ref, da_ref, zb_ref, db_ref, kv_ref = outs
    mine = place_ref[0]

    def put(out, head, sub):
        for which, ref in enumerate((q_ref, d_ref)):
            for h in range(SUB):
                at = pl.multiple_of(((head * 2 + sub) * SUB + h) * HD, HD)
                out[which, h] = ref[:, pl.ds(at, HD)]

    for sub in range(2):
        put(own_ref.at[sub], mine, sub)
        put(x_ref.at[sub], mine ^ 2, sub)
    put(za_ref, mine ^ 1, 0)
    put(da_ref, mine ^ 3, 0)
    put(zb_ref, mine ^ 1, 1)
    put(db_ref, mine ^ 3, 1)
    pos = pos_ref[...]
    high = jnp.broadcast_to((pos >> 7).astype(f32), (EXTRA, BLK)).astype(bf16)
    low = jnp.broadcast_to((pos & 127).astype(f32), (EXTRA, BLK)).astype(bf16)
    n = kv_ref.shape[0]
    for i in range(n):
        head = (i // (n // 2)) * 2 + i % 2
        cols = slice(head * HD, (head + 1) * HD)
        kv_ref[i, :BLK, :HD] = k_ref[:, cols]
        kv_ref[i, :BLK, HD:] = v_ref[:, cols]
        kv_ref[i, BLK:, :HD] = high
        kv_ref[i, BLK:, HD:] = low


def pack(place, query, grad_out, keys, values, positions, n):
    one = shape((2, SUB, BLK, HD), bf16)
    both = shape((2, 2, SUB, BLK, HD), bf16)
    return pl.pallas_call(
        pack_kernel,
        out_shape=(both, both, one, one, one, one, shape((n, BLK + EXTRA, 2 * HD), bf16)),
        in_specs=[SMEM] + [VMEM] * 5,
        out_specs=(VMEM,) * 7,
        compiler_params=params(24),
        cost_estimate=pl.CostEstimate(flops=0, bytes_accessed=6 << 20, transcendentals=0),
        name="pack",
    )(place, query, grad_out, keys, values, positions)


def attend_kernel(
    blocks_ref, own_ref, x_ref, za_ref, da_ref, zb_ref, db_ref, kv_hbm, table_ref, ks_ref, qs_ref,
    go_ref, gx_ref, gza_ref, gda_ref, gzb_ref, gdb_ref, term_ref, dkv_ref,
    s_scr, p_scr, qd_scr, kv_ref, cs_ref, kr_ref, kt_ref, q_scr, qt_scr, dt_scr, dq_scr, m_scr, l_scr, e_scr,
    gq_scr, dk_ref, dv_ref, tq_ref, sems, kv_sem,
):
    n = kv_ref.shape[0]
    kv_copy = pltpu.make_async_copy(kv_hbm, kv_ref, kv_sem)
    kv_copy.start()
    first, second = pl.ds(0, SUB), pl.ds(SUB, SUB)
    copies = [
        pltpu.make_async_copy(src, qd_scr.at[u, :, heads], sems.at[i])
        for i, (src, u, heads) in enumerate((
            (own_ref.at[0], 0, first), (own_ref.at[1], 0, second),
            (x_ref.at[0], 1, first), (x_ref.at[1], 1, second),
            (za_ref, 2, first), (zb_ref, 2, second),
            (da_ref, 3, first), (db_ref, 3, second),
        ))
    ]
    for copy in copies:
        copy.start()
    dk_ref[...] = jnp.zeros_like(dk_ref)
    dv_ref[...] = jnp.zeros_like(dv_ref)
    tq_ref[...] = jnp.zeros_like(tq_ref)
    sign = jnp.where(lax.broadcasted_iota(jnp.int32, (BLK, HD), 1) < HD // 2, -1.0, 1.0)
    row = lax.broadcasted_iota(jnp.int32, (BLK, BLK), 0).astype(f32)
    kv_copy.wait()

    def pick(i, part):
        pos = kv_ref[i, BLK : BLK + EXTRA, part * HD : (part + 1) * HD].astype(f32)[:1]
        hot = jnp.where(row == pos, 1.0, 0.0).T.astype(bf16)
        got = jnp.dot(hot, table_ref[part], preferred_element_type=f32)
        got = got[:, : 2 * HD] + got[:, 2 * HD :]
        return got[:, :HD], got[:, HD:]

    per = KEYS // BLK

    def ready(w, carry):
        for j in range(per):
            i = w * per + j
            at = pl.ds(pl.multiple_of(i * BLK, BLK), BLK)
            ch, sh = pick(i, 0)
            cl, sl = pick(i, 1)
            c = ch * cl - sh * sl
            s = (sh * cl + ch * sl) * sign
            cs_ref[at, :HD] = c
            cs_ref[at, HD:] = s
            r = turn(kv_ref[i, :BLK, :HD].astype(f32) * ks_ref[...], c, s)
            kr_ref[at, :] = r.astype(bf16)
            kt_ref[w, :, j * BLK : (j + 1) * BLK] = r.T.astype(bf16)
        return carry

    lax.fori_loop(0, n // per, ready, 0)
    for copy in copies:
        copy.wait()
    sub8 = lax.broadcasted_iota(jnp.int32, (8, ROWS), 0)
    lane = lax.broadcasted_iota(jnp.int32, (8, ROWS), 1)
    group = lax.broadcasted_iota(jnp.int32, (CHUNK // 8, 8, ROWS), 0) * 8

    def unit(u, carry):
        b0, b1 = blocks_ref[2 * u], blocks_ref[2 * u + 1]
        tabs = []
        for b in (b0, b1):
            toks = pl.ds(pl.multiple_of(b * BLK, BLK), BLK)
            tabs.append((cs_ref[toks, :HD], cs_ref[toks, HD:]))
        for h in range(2 * SUB):
            cols = slice(h * BLK, (h + 1) * BLK)
            r = turn(qd_scr[u, 0, h].astype(f32) * qs_ref[h : h + 1, :], *tabs[h // SUB])
            q_scr[cols, :] = r.astype(bf16)
            qt_scr[:, cols] = r.T.astype(bf16)
            dt_scr[:, cols] = qd_scr[u, 1, h].astype(f32).T.astype(bf16)
        dq_scr[...] = jnp.zeros_like(dq_scr)
        token = jnp.where(lane < ROWS // 2, b0, b1) * BLK + (lane & (BLK - 1)) - sub8
        steps = jnp.maximum(b0, b1) // per + 1

        def look(w, stats):
            m, l, d = stats
            for j in range(KEYS // CHUNK):
                at = pl.ds(pl.multiple_of(w * KEYS + j * CHUNK, CHUNK), CHUNK)
                vals = kv_ref[pl.ds(w * per + j * (CHUNK // BLK), CHUNK // BLK), :BLK, HD:]
                s = jnp.dot(kr_ref[at, :], qt_scr[...], preferred_element_type=f32)
                dp = jnp.dot(vals.reshape(CHUNK, HD), dt_scr[...], preferred_element_type=f32)
                p_scr[at, :] = dp
                s3 = s.reshape(CHUNK // 8, 8, ROWS)
                dp3 = dp.reshape(CHUNK // 8, 8, ROWS)
                s3 = jnp.where(group <= (token - (w * KEYS + j * CHUNK))[None], s3, NEG)
                s_scr[at, :] = s3.reshape(CHUNK, ROWS)
                mn = jnp.maximum(m, jnp.max(s3, axis=0))
                a = jnp.exp2((m - mn) * EXP2)
                e = jnp.exp2((s3 - mn[None]) * EXP2)
                m, l, d = mn, l * a + jnp.sum(e, axis=0), d * a + jnp.sum(e * dp3, axis=0)
            return m, l, d

        zero = jnp.zeros((8, ROWS), f32)
        m, l, d = lax.fori_loop(0, steps, look, (zero + NEG, zero, zero))
        top = jnp.max(m, axis=0, keepdims=True)
        w = jnp.exp2((m - top) * EXP2)
        total = jnp.sum(l * w, axis=0, keepdims=True)
        delta = jnp.sum(d * w, axis=0, keepdims=True) / total
        shift = top * EXP2 + jnp.log2(total)
        m_scr[...] = jnp.broadcast_to(shift, m_scr.shape)
        e_scr[...] = jnp.broadcast_to(delta, e_scr.shape)

        def back(w, carry):
            shift, delta = m_scr[...][None], e_scr[...][None]
            dq = dq_scr[...]
            for j in range(KEYS // CHUNK):
                at = pl.ds(pl.multiple_of(w * KEYS + j * CHUNK, CHUNK), CHUNK)
                s3 = s_scr[at, :].reshape(CHUNK // 8, 8, ROWS)
                dp3 = p_scr[at, :].reshape(CHUNK // 8, 8, ROWS)
                p = jnp.exp2(s3 * EXP2 - shift)
                ds = (p * (dp3 - delta)).reshape(CHUNK, ROWS).astype(bf16)
                p = p.reshape(CHUNK, ROWS).astype(bf16)
                dv_ref[at, :] += jnp.dot(p, qd_scr[u, 1].reshape(ROWS, HD), preferred_element_type=f32)
                dk_ref[at, :] += jnp.dot(ds, q_scr[...], preferred_element_type=f32)
                dq = dq + jnp.dot(
                    kt_ref[w, :, j * CHUNK : (j + 1) * CHUNK], ds, preferred_element_type=f32
                )
            dq_scr[...] = dq
            return carry

        lax.fori_loop(0, steps, back, 0)

        for h in range(2 * SUB):
            cos, sin = tabs[h // SUB]
            g = (dq_scr[:, h * BLK : (h + 1) * BLK] * FACTOR).T.astype(bf16).astype(f32)
            g = unturn(g, cos, sin)
            gq_scr[u, h] = (g * qs_ref[h : h + 1, :]).astype(bf16)
            tq_ref[h : h + 1, :] += jnp.sum(g * qd_scr[u, 0, h].astype(f32), axis=0, keepdims=True)
        return carry

    lax.fori_loop(0, 4, unit, 0)
    copies = [
        pltpu.make_async_copy(gq_scr.at[u, heads], dst, sems.at[i])
        for i, (dst, u, heads) in enumerate((
            (go_ref.at[0], 0, first), (go_ref.at[1], 0, second),
            (gx_ref.at[0], 1, first), (gx_ref.at[1], 1, second),
            (gza_ref, 2, first), (gzb_ref, 2, second),
            (gda_ref, 3, first), (gdb_ref, 3, second),
        ))
    ]
    for copy in copies:
        copy.start()

    def finish(c, tk):
        at = pl.ds(pl.multiple_of(c * BLK, BLK), BLK)
        g = dk_ref[at, :] * FACTOR
        dkv_ref[c, :BLK, :HD] = g.astype(bf16)
        dkv_ref[c, :BLK, HD:] = dv_ref[at, :].astype(bf16)
        dkv_ref[c, BLK:, :] = jnp.zeros((EXTRA, 2 * HD), bf16)
        g = unturn(g, cs_ref[at, :HD], cs_ref[at, HD:])
        return tk + jnp.sum(g * kv_ref[c, :BLK, :HD].astype(f32), axis=0, keepdims=True)

    tk = lax.fori_loop(0, n, finish, jnp.zeros((1, HD), f32))
    terms = jnp.concatenate([tq_ref[...], jnp.broadcast_to(tk, (8, HD))], axis=0)
    for j in range(term_ref.shape[0]):
        term_ref[j] = terms
    for copy in copies:
        copy.wait()


def attend(blocks, parts, kv, table, ks, qs, copies_of_term):
    n = kv.shape[0]
    length = n * BLK
    one, both = shape((SUB, BLK, HD), bf16), shape((2, SUB, BLK, HD), bf16)
    pairs = 4 * ROWS * length // 2
    return pl.pallas_call(
        attend_kernel,
        out_shape=(
            both, both, one, one, one, one,
            shape((copies_of_term, 2 * SUB + 8, HD), f32),
            shape(kv.shape, bf16),
        ),
        in_specs=[SMEM] + [ANY] * 7 + [VMEM] * 3,
        out_specs=(ANY,) * 6 + (VMEM,) * 2,
        scratch_shapes=[
            pltpu.VMEM((length, ROWS), f32),
            pltpu.VMEM((length, ROWS), f32),
            pltpu.VMEM((4, 2, 2 * SUB, BLK, HD), bf16),
            pltpu.VMEM(kv.shape, bf16),
            pltpu.VMEM((length, 2 * HD), f32),
            pltpu.VMEM((length, HD), bf16),
            pltpu.VMEM((length // KEYS, HD, KEYS), bf16),
            pltpu.VMEM((ROWS, HD), bf16),
            pltpu.VMEM((HD, ROWS), bf16),
            pltpu.VMEM((HD, ROWS), bf16),
            pltpu.VMEM((HD, ROWS), f32),
            pltpu.VMEM((8, ROWS), f32),
            pltpu.VMEM((8, ROWS), f32),
            pltpu.VMEM((8, ROWS), f32),
            pltpu.VMEM((4, 2 * SUB, BLK, HD), bf16),
            pltpu.VMEM((length, HD), f32),
            pltpu.VMEM((length, HD), f32),
            pltpu.VMEM((2 * SUB, HD), f32),
            pltpu.SemaphoreType.DMA((8,)),
            pltpu.SemaphoreType.DMA,
        ],
        compiler_params=params(44),
        cost_estimate=pl.CostEstimate(flops=pairs * HD * 20, bytes_accessed=8 << 20, transcendentals=pairs * 2),
        name="attend",
    )(blocks, *parts, kv, table, ks, qs)


def add_kernel(term_ref, dkv_in, dkv_ref, pair, sems):
    total = jnp.sum(term_ref[...], axis=0)
    high = total.astype(bf16)
    pair[:, :HD] = high
    pair[:, HD:] = (total - high.astype(f32)).astype(bf16)
    copies = [
        pltpu.make_async_copy(pair, dkv_ref.at[i, pl.ds(BLK, EXTRA)], sems.at[i])
        for i in range(dkv_ref.shape[0])
    ]
    for copy in copies:
        copy.start()
    for copy in copies:
        copy.wait()


def add(term, dkv):
    return pl.pallas_call(
        add_kernel,
        out_shape=shape(dkv.shape, bf16),
        in_specs=[VMEM, ANY],
        out_specs=ANY,
        scratch_shapes=[pltpu.VMEM((EXTRA, 2 * HD), bf16), pltpu.SemaphoreType.DMA((dkv.shape[0],))],
        input_output_aliases={1: 0},
        compiler_params=params(8),
        name="add",
    )(term, dkv)


def unpack_kernel(place_ref, own_ref, x_ref, za_ref, da_ref, zb_ref, db_ref, out_ref):
    mine = place_ref[0]

    def put(src, head, sub):
        for h in range(SUB):
            at = pl.multiple_of(((head * 2 + sub) * SUB + h) * HD, HD)
            out_ref[:, pl.ds(at, HD)] = src[h]

    for sub in range(2):
        put(own_ref.at[sub], mine, sub)
        put(x_ref.at[sub], mine ^ 2, sub)
    put(za_ref, mine ^ 1, 0)
    put(da_ref, mine ^ 3, 0)
    put(zb_ref, mine ^ 1, 1)
    put(db_ref, mine ^ 3, 1)


def unpack(place, parts):
    return pl.pallas_call(
        unpack_kernel,
        out_shape=shape((BLK, HQ * HD), bf16),
        in_specs=[SMEM] + [VMEM] * 6,
        out_specs=VMEM,
        compiler_params=params(8),
        cost_estimate=pl.CostEstimate(flops=0, bytes_accessed=2 << 20, transcendentals=0),
        name="unpack",
    )(place, *parts)


def final_kernel(dkv_ref, tab, ks_ref, gk_ref, gv_ref, tq_ref, tk_ref):
    n = dkv_ref.shape[0]
    for head in range(HK):
        first = (head // 2) * (n // 2) + head % 2
        got = jnp.zeros((BLK + EXTRA, 2 * HD), f32)
        for i in range(first, first + n // 2, 2):
            got = got + dkv_ref[i].astype(f32)
        cols = slice(head * HD, (head + 1) * HD)
        g = unturn(got[:BLK, :HD].astype(bf16).astype(f32), tab[:, :HD], tab[:, HD:])
        gk_ref[:, cols] = (g * ks_ref[head : head + 1, :]).astype(bf16)
        gv_ref[:, cols] = got[:BLK, HD:].astype(bf16)
        term = got[BLK:, :HD] + got[BLK:, HD:]
        tq_ref[head * 2 * SUB : (head + 1) * 2 * SUB, :] = term[: 2 * SUB]
        tk_ref[head : head + 1, :] = term[2 * SUB : 2 * SUB + 1]


def final(dkv, table, ks):
    return pl.pallas_call(
        final_kernel,
        out_shape=(
            shape((BLK, HK * HD), bf16),
            shape((BLK, HK * HD), bf16),
            shape((HQ, HD), f32),
            shape((HK, HD), f32),
        ),
        in_specs=[VMEM] * 3,
        out_specs=(VMEM,) * 4,
        compiler_params=params(8),
        name="final",
    )(dkv, table, ks)


def shards(query, keys, values, grad_out, positions, q_scale, k_scale):
    n = lax.axis_size("seq")
    half = n // 2
    me = lax.axis_index("seq")
    x, z = me // half, me % half
    odd = z % 2
    kind = x * 2 + odd
    place = jnp.stack([kind, me]).astype(jnp.int32)
    za = z + 1 - 2 * odd
    zb = (z - 1 + 2 * odd) % half

    def pairs(flip, step):
        out = []
        for i in range(n):
            xi, zi = i // half, i % half
            zo = (zi + step * (1 - 2 * (zi % 2))) % half
            out.append((i, (xi ^ flip) * half + zo))
        return out

    def send(a, flip, step):
        return lax.ppermute(a, "seq", pairs(flip, step))

    own, to_x, to_za, to_da, to_zb, to_db, kv = pack(
        place, query[0], grad_out[0], keys[0], values[0], positions, n
    )
    kv = lax.all_to_all(kv, "seq", 0, 0, tiled=True)
    in_x = send(to_x, 1, 0)
    in_za, in_da = send(to_za, 0, 1), send(to_da, 1, 1)
    in_zb, in_db = send(to_zb, 0, -1), send(to_db, 1, -1)

    q_gain = lax.dynamic_slice_in_dim(q_scale.reshape(HK, 2 * SUB, HD), kind, 1, 0)[0]
    k_gain = lax.dynamic_slice_in_dim(k_scale.reshape(HK, HD), kind, 1, 0)
    pair = lambda side: [side * half + za, side * half + zb]
    blocks = jnp.stack([me, me, me ^ half, me ^ half, *pair(x), *pair(1 - x)]).astype(jnp.int32)
    go, gx, gza, gda, gzb, gdb, term, dkv = attend(
        blocks,
        (own, in_x, in_za, in_da, in_zb, in_db),
        kv,
        angle_tables(),
        k_gain,
        q_gain,
        lax.axis_size("dp"),
    )

    term = lax.all_to_all(term, "dp", 0, 0, tiled=True)
    back = (go, send(gx, 1, 0), send(gza, 0, 1), send(gda, 1, 1), send(gzb, 0, -1), send(gdb, 1, -1))
    dkv, back = lax.optimization_barrier((add(term, dkv), back))
    dkv = lax.all_to_all(dkv, "seq", 0, 0, tiled=True)
    grad_query = unpack(place, back)
    grad_keys, grad_values, total_q, total_k = final(
        dkv, full_table(positions[0]), k_scale.reshape(HK, HD)
    )
    return (
        grad_query[None],
        grad_keys[None],
        grad_values[None],
        total_q.reshape(HQ * HD),
        total_k.reshape(HK * HD),
    )


def solution(mesh):
    return jax.shard_map(
        shards,
        mesh=mesh,
        in_specs=(
            P("dp", "seq", None),
            P("dp", "seq", None),
            P("dp", "seq", None),
            P("dp", "seq", None),
            P("dp", "seq"),
            P(),
            P(),
        ),
        out_specs=(P("dp", "seq", None), P("dp", "seq", None), P("dp", "seq", None), P(), P()),
        check_vma=False,
    )
```

time: 438 us -> 165 us (0.38); the launches traced: 431 us -> 164 us
  blocking collectives: 98.6 us -> 0 us
  waiting for transfers between devices: 149 us -> 55.8 us
  local copies, waits for them, and re-layouts: 58.5 us -> 7.97 us
  other arithmetic: 38.9 us -> 1.16 us
  Pallas kernels: 0 us -> 34.2 us
  matrix products: 33.4 us -> 0 us
  starting transfers between devices: 50.5 us -> 63.4 us
    all_to_all x7 -> x3, waiting for transfers between devices: 149 us -> 25.2 us  [the longest x1 25.2 us: shards(): dkv = lax.all_to_all(dkv, 'seq', 0, 0, tiled=True)]
    psum x1 -> x0, blocking collectives: 98.6 us -> none  [shards(): total_q, total_k = lax.psum((term_q, term_k), ('dp', 'seq'))]
    pallas_call x0 -> x5, Pallas kernels: none -> 34.2 us  [the longest x1 28.3 us: attend(): pl.pallas_call(attend_kernel, out_shape=(both, both, one, one, one, one,...]
    dot_general x48 -> x0, matrix products: 33.4 us -> none  [the longest x8 8.26 us: attend_backward(): jnp.einsum('shqk,skd->sqhd', dscore, k_blk, preferred_element_type=jnp.fl...]
    ppermute x0 -> x10, starting transfers between devices: none -> 33.1 us  [send(): return lax.ppermute(a, 'seq', pairs(flip, step))]
    ppermute x0 -> x10, waiting for transfers between devices: none -> 30.6 us  [send(): return lax.ppermute(a, 'seq', pairs(flip, step))]
    reduce_sum x14 -> x0, other arithmetic: 21.8 us -> none  [the longest x2 8.89 us: shards(): dv_sum = dv_tok.reshape(seq_here, tokens_here, HK, group, HD).sum(axis=3)]
    all_to_all x7 -> x3, starting transfers between devices: 50.5 us -> 30.2 us  [the longest x1 12.2 us: shards(): term = lax.all_to_all(term, 'dp', 0, 0, tiled=True)]
  transfers between devices with their start and end apart: 7 -> 13, of which waited for: 7 -> 5; matrix products, arithmetic and copies ran while one was open for 15% -> 1% of each run, Pallas kernels for 0% -> 2%
where the time goes in v1:
time: 165 us; the launch traced here: 164 us
  starting transfers between devices  63.4 us (38%)
  waiting for transfers between devices  55.8 us (34%)
  Pallas kernels  34.2 us (21%)
  local copies, waits for them, and re-layouts  7.97 us (5%)
    ppermute x10, starting transfers between devices, send(): return lax.ppermute(a, 'seq', pairs(flip, step))  33.1 us
    ppermute x10, waiting for transfers between devices, send(): return lax.ppermute(a, 'seq', pairs(flip, step))  30.6 us
    pallas_call x1, Pallas kernels, attend(): pl.pallas_call(attend_kernel, out_shape=(both, both, one, one, one, one,...  28.3 us
    all_to_all x1, waiting for transfers between devices, shards(): dkv = lax.all_to_all(dkv, 'seq', 0, 0, tiled=True)  25.2 us
    all_to_all x1, starting transfers between devices, shards(): term = lax.all_to_all(term, 'dp', 0, 0, tiled=True)  12.2 us
    all_to_all x1, starting transfers between devices, shards(): kv = lax.all_to_all(kv, 'seq', 0, 0, tiled=True)  12 us
    unnamed x24, local copies, waits for them, and re-layouts  7.88 us
    all_to_all x1, starting transfers between devices, shards(): dkv = lax.all_to_all(dkv, 'seq', 0, 0, tiled=True)  6.05 us
  transfers between devices with their start and end apart: 13, of which 5 were waited for; matrix products, arithmetic and copies ran while one was open for 1% of the time, Pallas kernels for 2%

profile of v1, /device:TPU:1, one launch (start us, length us, event | category | flops | bytes accessed | tf_op | source)
XLA Modules:
  0.0 163.5 jit_solution(11195327321883136575)
XLA Ops:
  0.8 1.2 copy-done.1
  2.0 1.2 copy-done.2
  3.2 0.9 copy-done.3
  5.7 2.4 %pack.1 = (bf16[2,2,4,128,128]{4,3,2,1,0:T(8,128)(2,1)S(1)}, bf16[2,2,4,128,128]{4,3,2,1,0:T(8,128)(2,1)S(1)}, bf16[2,4,128,128]{3,2,1,0:T(8,128)(2,1)}, bf16[2,...) custom-call(s32[2]{0:T(128)S(1)} %pad_add_fusion.place_ref, ...), custom_call_target="tpu_custom_call" | custom-call | bytes 6291456 | tf_op jit(solution)/shard_map/pack/pallas_call | solution.py:104
  8.1 12.0 %all-to-all-start = ((bf16[16,144,256]{2,1,0:T(8,128)(2,1)}), bf16[16,144,256]{2,1,0:T(8,128)(2,1)S(1)}, u32[]{:S(2)}, u32[]{:S(2)}) async-start(bf16[16,144,256]{2,1,0:T(8,128)(2,1)} %get-tuple-element.37), calls=%async_computation | async-start | bytes 2359296 | tf_op jit(solution)/shard_map/all_to_all | solution.py:432
  20.1 3.3 %collective-permute-start = (bf16[2,2,4,128,128]{4,3,2,1,0:T(8,128)(2,1)S(1)}, bf16[2,2,4,128,128]{4,3,2,1,0:T(8,128)(2,1)S(1)}, u32[]{:S(2)}, u32[]{:S(2)}) collective-permute-start(bf16[2,2,4,128,128]{4,3,2,1,0:T(8,128)(2,1)S(1)} %get-tuple-element.32), channel_id=1, source_target_pairs={{0,8},{1,9},{2,10},{3,11},{4,12},{5,13},{6,14},{7,15},{8,0},{9,1},... | collective-permute-start | bytes 1572872 | tf_op jit(solution)/shard_map/ppermute | solution.py:427
  23.4 3.1 %collective-permute-start.1 = (bf16[2,4,128,128]{3,2,1,0:T(8,128)(2,1)}, bf16[2,4,128,128]{3,2,1,0:T(8,128)(2,1)S(1)}, u32[]{:S(2)}, u32[]{:S(2)}) collective-permute-start(bf16[2,4,128,128]{3,2,1,0:T(8,128)(2,1)} %get-tuple-element.33), channel_id=1, source_target_pairs={{0,1},{1,0},{2,3},{3,2},{4,5},{5,4},{6,7},{7,6},{8,9},{9,8},{10,11... | collective-permute-start | bytes 786440 | tf_op jit(solution)/shard_map/ppermute | solution.py:427
  26.5 2.0 %collective-permute-start.2 = (bf16[2,4,128,128]{3,2,1,0:T(8,128)(2,1)}, bf16[2,4,128,128]{3,2,1,0:T(8,128)(2,1)}, u32[]{:S(2)}, u32[]{:S(2)}) collective-permute-start(bf16[2,4,128,128]{3,2,1,0:T(8,128)(2,1)} %get-tuple-element.34), channel_id=1, source_target_pairs={{0,9},{1,8},{2,11},{3,10},{4,13},{5,12},{6,15},{7,14},{8,1},{9,0},... | collective-permute-start | bytes 786440 | tf_op jit(solution)/shard_map/ppermute | solution.py:427
  28.5 4.5 %collective-permute-start.3 = (bf16[2,4,128,128]{3,2,1,0:T(8,128)(2,1)}, bf16[2,4,128,128]{3,2,1,0:T(8,128)(2,1)}, u32[]{:S(2)}, u32[]{:S(2)}) collective-permute-start(bf16[2,4,128,128]{3,2,1,0:T(8,128)(2,1)} %get-tuple-element.35), channel_id=1, source_target_pairs={{0,7},{1,2},{2,1},{3,4},{4,3},{5,6},{6,5},{7,0},{8,15},{9,10},{10,... | collective-permute-start | bytes 786440 | tf_op jit(solution)/shard_map/ppermute | solution.py:427
  33.0 3.1 %collective-permute-start.4 = (bf16[2,4,128,128]{3,2,1,0:T(8,128)(2,1)}, bf16[2,4,128,128]{3,2,1,0:T(8,128)(2,1)}, u32[]{:S(2)}, u32[]{:S(2)}) collective-permute-start(bf16[2,4,128,128]{3,2,1,0:T(8,128)(2,1)} %get-tuple-element.36), channel_id=1, source_target_pairs={{0,15},{1,10},{2,9},{3,12},{4,11},{5,14},{6,13},{7,8},{8,7},{9,2},... | collective-permute-start | bytes 786440 | tf_op jit(solution)/shard_map/ppermute | solution.py:427
  36.9 15.9 %collective-permute-done.1.za_ref = bf16[2,4,128,128]{3,2,1,0:T(8,128)(2,1)S(1)} collective-permute-done((bf16[2,4,128,128]{3,2,1,0:T(8,128)(2,1)}, bf16[2,4,128,128]{3,2,1,0:T(8,128)(2,1)S(1)}, u32[]{:S(2)}, u32[]{:S(2)}) %collective-permute-start.1) | collective-permute-done | bytes 262176 | tf_op jit(solution)/shard_map/ppermute | solution.py:427
  53.6 9.7 %collective-permute-done.2.da_ref = bf16[2,4,128,128]{3,2,1,0:T(8,128)(2,1)} collective-permute-done((bf16[2,4,128,128]{3,2,1,0:T(8,128)(2,1)}, bf16[2,4,128,128]{3,2,1,0:T(8,128)(2,1)}, u32[]{:S(2)}, u32[]{:S(2)}) %collective-permute-start.2) | collective-permute-done | bytes 262176 | tf_op jit(solution)/shard_map/ppermute | solution.py:427
  63.3 0.9 copy-done.9
  64.2 28.3 %attend.1 = (bf16[2,4,128,128]{3,2,1,0:T(8,128)(2,1)S(1)}, bf16[2,4,128,128]{3,2,1,0:T(8,128)(2,1)S(1)}, bf16[4,128,128]{2,1,0:T(8,128)(2,1)S(1)}, bf16[4,128,12...) custom-call(s32[8]{0:T(128)S(1)} %stack.43.blocks_ref, ...), custom_call_target="tpu_custom_call" | custom-call | flops 10737418240 | bytes 8388608 | tf_op jit(solution)/shard_map/attend/pallas_call | solution.py:281
  93.9 12.2 %all-to-all-start.1 = ((f32[32,16,128]{2,1,0:T(8,128)}), f32[32,16,128]{2,1,0:T(8,128)S(1)}, u32[]{:S(2)}, u32[]{:S(2)}) async-start(f32[32,16,128]{2,1,0:T(8,128)} %get-tuple-element.38), calls=%async_computation.1 | async-start | bytes 524288 | tf_op jit(solution)/shard_map/all_to_all | solution.py:451
  106.0 1.9 %collective-permute-start.5 = (bf16[2,4,128,128]{3,2,1,0:T(8,128)(2,1)S(1)}, bf16[2,4,128,128]{3,2,1,0:T(8,128)(2,1)S(1)}, u32[]{:S(2)}, u32[]{:S(2)}) collective-permute-start(bf16[2,4,128,128]{3,2,1,0:T(8,128)(2,1)S(1)} %get-tuple-element.41), channel_id=1, source_target_pairs={{0,8},{1,9},{2,10},{3,11},{4,12},{5,13},{6,14},{7,15},{8,0},{9,1},... | collective-permute-start | bytes 786440 | tf_op jit(solution)/shard_map/ppermute | solution.py:427
  107.9 1.9 %collective-permute-start.6 = (bf16[4,128,128]{2,1,0:T(8,128)(2,1)}, bf16[4,128,128]{2,1,0:T(8,128)(2,1)S(1)}, u32[]{:S(2)}, u32[]{:S(2)}) collective-permute-start(bf16[4,128,128]{2,1,0:T(8,128)(2,1)} %copy-done.11), channel_id=1, source_target_pairs={{0,1},{1,0},{2,3},{3,2},{4,5},{5,4},{6,7},{7,6},{8,9},{9,8},{10,11... | collective-permute-start | bytes 393224 | tf_op jit(solution)/shard_map/ppermute | solution.py:427
  109.9 4.5 %collective-permute-start.7 = (bf16[4,128,128]{2,1,0:T(8,128)(2,1)}, bf16[4,128,128]{2,1,0:T(8,128)(2,1)S(1)}, u32[]{:S(2)}, u32[]{:S(2)}) collective-permute-start(bf16[4,128,128]{2,1,0:T(8,128)(2,1)} %copy-done.10), channel_id=1, source_target_pairs={{0,9},{1,8},{2,11},{3,10},{4,13},{5,12},{6,15},{7,14},{8,1},{9,0},... | collective-permute-start | bytes 393224 | tf_op jit(solution)/shard_map/ppermute | solution.py:427
  114.4 6.9 %collective-permute-start.8 = (bf16[4,128,128]{2,1,0:T(8,128)(2,1)S(1)}, bf16[4,128,128]{2,1,0:T(8,128)(2,1)S(1)}, u32[]{:S(2)}, u32[]{:S(2)}) collective-permute-start(bf16[4,128,128]{2,1,0:T(8,128)(2,1)S(1)} %get-tuple-element.44), channel_id=1, source_target_pairs={{0,7},{1,2},{2,1},{3,4},{4,3},{5,6},{6,5},{7,0},{8,15},{9,10},{10,... | collective-permute-start | bytes 393224 | tf_op jit(solution)/shard_map/ppermute | solution.py:427
  121.3 1.9 %collective-permute-start.9 = (bf16[4,128,128]{2,1,0:T(8,128)(2,1)S(1)}, bf16[4,128,128]{2,1,0:T(8,128)(2,1)S(1)}, u32[]{:S(2)}, u32[]{:S(2)}) collective-permute-start(bf16[4,128,128]{2,1,0:T(8,128)(2,1)S(1)} %get-tuple-element.45), channel_id=1, source_target_pairs={{0,15},{1,10},{2,9},{3,12},{4,11},{5,14},{6,13},{7,8},{8,7},{9,2},... | collective-permute-start | bytes 393224 | tf_op jit(solution)/shard_map/ppermute | solution.py:427
  124.2 4.9 %collective-permute-done.9.db_ref = bf16[4,128,128]{2,1,0:T(8,128)(2,1)S(1)} collective-permute-done((bf16[4,128,128]{2,1,0:T(8,128)(2,1)S(1)}, bf16[4,128,128]{2,1,0:T(8,128)(2,1)S(1)}, u32[]{:S(2)}, u32[]{:S(2)}) %collective-permute-start.9) | collective-permute-done | bytes 131104 | tf_op jit(solution)/shard_map/ppermute | solution.py:427
  129.1 6.0 %all-to-all-start.2 = ((bf16[16,144,256]{2,1,0:T(8,128)(2,1)}), bf16[16,144,256]{2,1,0:T(8,128)(2,1)S(1)}, u32[]{:S(2)}, u32[]{:S(2)}) async-start(bf16[16,144,256]{2,1,0:T(8,128)(2,1)} %add.51), calls=%async_computation.2 | async-start | bytes 2359296 | tf_op jit(solution)/shard_map/all_to_all | solution.py:454
  135.7 1.8 %unpack.1 = bf16[128,4096]{1,0:T(8,128)(2,1)} custom-call(s32[2]{0:T(128)S(1)} %pad_add_fusion.place_ref, bf16[2,4,128,128]{3,2,1,0:T(8,128)(2,1)S(1)} %get-tuple-element.46.own_ref, bf16[2,4,128,128]{3,2,1,0:T(8,128)(2,1)S(1)} %collective-permute-done.5.x_ref, bf16[4,128,128]{2,1,0:T(8,128)(2,1)S(1)} %collective-permute-done.6.za_ref, ...), custom_call_target="tpu_custom_call" | custom-call | bytes 2097152 | tf_op jit(solution)/shard_map/unpack/pallas_call | solution.py:364
  137.5 25.2 %all-to-all-done.2.dkv_ref = bf16[16,144,256]{2,1,0:T(8,128)(2,1)S(1)} async-done(((bf16[16,144,256]{2,1,0:T(8,128)(2,1)}), bf16[16,144,256]{2,1,0:T(8,128)(2,1)S(1)}, u32[]{:S(2)}, u32[]{:S(2)}) %all-to-all-start.2) | async-done | bytes 1179680 | tf_op jit(solution)/shard_map/all_to_all | solution.py:454
  (44 shorter events, 6.7 us)
Async XLA Ops:
  0.6 35.6 %copy-start = (f32[4096]{0:T(1024)S(1)}, f32[4096]{0:T(1024)}, u32[]{:S(2)}) copy-start(f32[4096]{0:T(1024)} %param.12) | copy-start | bytes 49156
  0.8 1.2 copy-start.1
  2.0 1.2 copy-start.2
  3.2 0.9 copy-start.3
  4.1 0.9 copy-start.4
  5.0 0.7 copy-start.6
  8.1 28.7 %copy-start.5 = (f32[512]{0:T(512)S(1)}, f32[512]{0:T(512)}, u32[]{:S(2)}) copy-start(f32[512]{0:T(512)} %param.13) | copy-start | bytes 6148
  8.1 55.2 %all-to-all-start = ((bf16[16,144,256]{2,1,0:T(8,128)(2,1)}), bf16[16,144,256]{2,1,0:T(8,128)(2,1)S(1)}, u32[]{:S(2)}, u32[]{:S(2)}) async-start(bf16[16,144,256]{2,1,0:T(8,128)(2,1)} %get-tuple-element.37), calls=%async_computation | async-start | bytes 2359296 | tf_op jit(solution)/shard_map/all_to_all | solution.py:432
  20.1 43.1 %collective-permute-start = (bf16[2,2,4,128,128]{4,3,2,1,0:T(8,128)(2,1)S(1)}, bf16[2,2,4,128,128]{4,3,2,1,0:T(8,128)(2,1)S(1)}, u32[]{:S(2)}, u32[]{:S(2)}) collective-permute-start(bf16[2,2,4,128,128]{4,3,2,1,0:T(8,128)(2,1)S(1)} %get-tuple-element.32), channel_id=1, source_target_pairs={{0,8},{1,9},{2,10},{3,11},{4,12},{5,13},{6,14},{7,15},{8,0},{9,1},... | collective-permute-start | bytes 1572872 | tf_op jit(solution)/shard_map/ppermute | solution.py:427
  23.4 29.5 %collective-permute-start.1 = (bf16[2,4,128,128]{3,2,1,0:T(8,128)(2,1)}, bf16[2,4,128,128]{3,2,1,0:T(8,128)(2,1)S(1)}, u32[]{:S(2)}, u32[]{:S(2)}) collective-permute-start(bf16[2,4,128,128]{3,2,1,0:T(8,128)(2,1)} %get-tuple-element.33), channel_id=1, source_target_pairs={{0,1},{1,0},{2,3},{3,2},{4,5},{5,4},{6,7},{7,6},{8,9},{9,8},{10,11... | collective-permute-start | bytes 786440 | tf_op jit(solution)/shard_map/ppermute | solution.py:427
  26.5 36.8 %collective-permute-start.2 = (bf16[2,4,128,128]{3,2,1,0:T(8,128)(2,1)}, bf16[2,4,128,128]{3,2,1,0:T(8,128)(2,1)}, u32[]{:S(2)}, u32[]{:S(2)}) collective-permute-start(bf16[2,4,128,128]{3,2,1,0:T(8,128)(2,1)} %get-tuple-element.34), channel_id=1, source_target_pairs={{0,9},{1,8},{2,11},{3,10},{4,13},{5,12},{6,15},{7,14},{8,1},{9,0},... | collective-permute-start | bytes 786440 | tf_op jit(solution)/shard_map/ppermute | solution.py:427
  28.5 34.7 %collective-permute-start.3 = (bf16[2,4,128,128]{3,2,1,0:T(8,128)(2,1)}, bf16[2,4,128,128]{3,2,1,0:T(8,128)(2,1)}, u32[]{:S(2)}, u32[]{:S(2)}) collective-permute-start(bf16[2,4,128,128]{3,2,1,0:T(8,128)(2,1)} %get-tuple-element.35), channel_id=1, source_target_pairs={{0,7},{1,2},{2,1},{3,4},{4,3},{5,6},{6,5},{7,0},{8,15},{9,10},{10,... | collective-permute-start | bytes 786440 | tf_op jit(solution)/shard_map/ppermute | solution.py:427
  33.0 30.3 %collective-permute-start.4 = (bf16[2,4,128,128]{3,2,1,0:T(8,128)(2,1)}, bf16[2,4,128,128]{3,2,1,0:T(8,128)(2,1)}, u32[]{:S(2)}, u32[]{:S(2)}) collective-permute-start(bf16[2,4,128,128]{3,2,1,0:T(8,128)(2,1)} %get-tuple-element.36), channel_id=1, source_target_pairs={{0,15},{1,10},{2,9},{3,12},{4,11},{5,14},{6,13},{7,8},{8,7},{9,2},... | collective-permute-start | bytes 786440 | tf_op jit(solution)/shard_map/ppermute | solution.py:427
  52.9 0.7 copy-start.8
  63.2 1.0 copy-start.9
  92.5 0.7 copy-start.10
  93.9 29.4 %all-to-all-start.1 = ((f32[32,16,128]{2,1,0:T(8,128)}), f32[32,16,128]{2,1,0:T(8,128)S(1)}, u32[]{:S(2)}, u32[]{:S(2)}) async-start(f32[32,16,128]{2,1,0:T(8,128)} %get-tuple-element.38), calls=%async_computation.1 | async-start | bytes 524288 | tf_op jit(solution)/shard_map/all_to_all | solution.py:451
  106.0 23.1 %collective-permute-start.5 = (bf16[2,4,128,128]{3,2,1,0:T(8,128)(2,1)S(1)}, bf16[2,4,128,128]{3,2,1,0:T(8,128)(2,1)S(1)}, u32[]{:S(2)}, u32[]{:S(2)}) collective-permute-start(bf16[2,4,128,128]{3,2,1,0:T(8,128)(2,1)S(1)} %get-tuple-element.41), channel_id=1, source_target_pairs={{0,8},{1,9},{2,10},{3,11},{4,12},{5,13},{6,14},{7,15},{8,0},{9,1},... | collective-permute-start | bytes 786440 | tf_op jit(solution)/shard_map/ppermute | solution.py:427
  107.9 16.2 %collective-permute-start.6 = (bf16[4,128,128]{2,1,0:T(8,128)(2,1)}, bf16[4,128,128]{2,1,0:T(8,128)(2,1)S(1)}, u32[]{:S(2)}, u32[]{:S(2)}) collective-permute-start(bf16[4,128,128]{2,1,0:T(8,128)(2,1)} %copy-done.11), channel_id=1, source_target_pairs={{0,1},{1,0},{2,3},{3,2},{4,5},{5,4},{6,7},{7,6},{8,9},{9,8},{10,11... | collective-permute-start | bytes 393224 | tf_op jit(solution)/shard_map/ppermute | solution.py:427
  109.9 14.3 %collective-permute-start.7 = (bf16[4,128,128]{2,1,0:T(8,128)(2,1)}, bf16[4,128,128]{2,1,0:T(8,128)(2,1)S(1)}, u32[]{:S(2)}, u32[]{:S(2)}) collective-permute-start(bf16[4,128,128]{2,1,0:T(8,128)(2,1)} %copy-done.10), channel_id=1, source_target_pairs={{0,9},{1,8},{2,11},{3,10},{4,13},{5,12},{6,15},{7,14},{8,1},{9,0},... | collective-permute-start | bytes 393224 | tf_op jit(solution)/shard_map/ppermute | solution.py:427
  114.4 9.8 %collective-permute-start.8 = (bf16[4,128,128]{2,1,0:T(8,128)(2,1)S(1)}, bf16[4,128,128]{2,1,0:T(8,128)(2,1)S(1)}, u32[]{:S(2)}, u32[]{:S(2)}) collective-permute-start(bf16[4,128,128]{2,1,0:T(8,128)(2,1)S(1)} %get-tuple-element.44), channel_id=1, source_target_pairs={{0,7},{1,2},{2,1},{3,4},{4,3},{5,6},{6,5},{7,0},{8,15},{9,10},{10,... | collective-permute-start | bytes 393224 | tf_op jit(solution)/shard_map/ppermute | solution.py:427
  121.3 7.8 %collective-permute-start.9 = (bf16[4,128,128]{2,1,0:T(8,128)(2,1)S(1)}, bf16[4,128,128]{2,1,0:T(8,128)(2,1)S(1)}, u32[]{:S(2)}, u32[]{:S(2)}) collective-permute-start(bf16[4,128,128]{2,1,0:T(8,128)(2,1)S(1)} %get-tuple-element.45), channel_id=1, source_target_pairs={{0,15},{1,10},{2,9},{3,12},{4,11},{5,14},{6,13},{7,8},{8,7},{9,2},... | collective-permute-start | bytes 393224 | tf_op jit(solution)/shard_map/ppermute | solution.py:427
  129.1 6.1 %copy-start.7 = (s32[1,128]{1,0:T(1,128)S(1)}, s32[1,128]{1,0:T(1,128)}, u32[]{:S(2)}) copy-start(s32[1,128]{1,0:T(1,128)} %pos_ref.1) | copy-start | bytes 1540
  129.1 33.5 %all-to-all-start.2 = ((bf16[16,144,256]{2,1,0:T(8,128)(2,1)}), bf16[16,144,256]{2,1,0:T(8,128)(2,1)S(1)}, u32[]{:S(2)}, u32[]{:S(2)}) async-start(bf16[16,144,256]{2,1,0:T(8,128)(2,1)} %add.51), calls=%async_computation.2 | async-start | bytes 2359296 | tf_op jit(solution)/shard_map/all_to_all | solution.py:454
  (1 other events, 0.7 us)

commit v2 on v1

--- a/solution.py
+++ b/solution.py
@@ -26,6 +26,7 @@
 VMEM = pl.BlockSpec(memory_space=pltpu.VMEM)
 SMEM = pl.BlockSpec(memory_space=pltpu.SMEM)
 ANY = pl.BlockSpec(memory_space=pl.ANY)
+HBM = pl.BlockSpec(memory_space=pltpu.HBM)
 
 
 def shape(dims, dtype):
@@ -42,6 +43,10 @@
 
 def unturn(x, c, s):
     return x * c - pltpu.roll(x, HD // 2, 1) * s
+
+
+def dot_t(a, b):
+    return lax.dot_general(a, b, (((1,), (1,)), ((), ())), preferred_element_type=f32)
 
 
 def two_parts(x):
@@ -68,23 +73,15 @@
     return jnp.concatenate([cosine, cosine, -sine, sine], axis=-1)
 
 
-def pack_kernel(place_ref, q_ref, d_ref, k_ref, v_ref, pos_ref, *outs):
-    own_ref, x_ref, za_ref, da_ref, zb_ref, db_ref, kv_ref = outs
-    mine = place_ref[0]
-
-    def put(out, head, sub):
-        for which, ref in enumerate((q_ref, d_ref)):
-            for h in range(SUB):
-                at = pl.multiple_of(((head * 2 + sub) * SUB + h) * HD, HD)
-                out[which, h] = ref[:, pl.ds(at, HD)]
-
-    for sub in range(2):
-        put(own_ref.at[sub], mine, sub)
-        put(x_ref.at[sub], mine ^ 2, sub)
-    put(za_ref, mine ^ 1, 0)
-    put(da_ref, mine ^ 3, 0)
-    put(zb_ref, mine ^ 1, 1)
-    put(db_ref, mine ^ 3, 1)
+def pack_kv_kernel(k_hbm, v_hbm, pos_hbm, kv_ref, k_ref, v_ref, pos_ref, sems):
+    copies = [
+        pltpu.make_async_copy(src, dst, sems.at[i])
+        for i, (src, dst) in enumerate(((k_hbm, k_ref), (v_hbm, v_ref), (pos_hbm, pos_ref)))
+    ]
+    for copy in copies:
+        copy.start()
+    for copy in copies:
+        copy.wait()
     pos = pos_ref[...]
     high = jnp.broadcast_to((pos >> 7).astype(f32), (EXTRA, BLK)).astype(bf16)
     low = jnp.broadcast_to((pos & 127).astype(f32), (EXTRA, BLK)).astype(bf16)
@@ -98,47 +95,62 @@
         kv_ref[i, BLK:, HD:] = low
 
 
-def pack(place, query, grad_out, keys, values, positions, n):
+def pack_kv(keys, values, positions, n):
+    return pl.pallas_call(
+        pack_kv_kernel,
+        out_shape=shape((n, BLK + EXTRA, 2 * HD), bf16),
+        in_specs=[HBM] * 3,
+        out_specs=VMEM,
+        scratch_shapes=[
+            pltpu.VMEM(keys.shape, bf16),
+            pltpu.VMEM(values.shape, bf16),
+            pltpu.VMEM(positions.shape, jnp.int32),
+            pltpu.SemaphoreType.DMA((3,)),
+        ],
+        compiler_params=params(60),
+        cost_estimate=pl.CostEstimate(flops=0, bytes_accessed=2 << 20, transcendentals=0),
+        name="pack_kv",
+    )(keys, values, positions)
+
+
+def pack_kernel(place_ref, q_ref, d_ref, own_ref, x_ref, za_ref, da_ref, zb_ref, db_ref, sems):
+    mine = place_ref[0]
+    targets = [
+        (x_ref.at[0], 2, 0), (x_ref.at[1], 2, 1), (za_ref, 1, 0), (da_ref, 3, 0), (zb_ref, 1, 1), (db_ref, 3, 1),
+        (own_ref.at[0], 0, 0), (own_ref.at[1], 0, 1),
+    ]
+    copies = []
+    for out, flip, sub in targets:
+        for which, ref in enumerate((q_ref, d_ref)):
+            for h in range(SUB):
+                at = pl.multiple_of((((mine ^ flip) * 2 + sub) * SUB + h) * HD, HD)
+                copies.append(
+                    pltpu.make_async_copy(ref.at[:, pl.ds(at, HD)], out.at[which, h], sems.at[len(copies)])
+                )
+                copies[-1].start()
+    for copy in copies:
+        copy.wait()
+
+
+def pack(place, query, grad_out):
     one = shape((2, SUB, BLK, HD), bf16)
     both = shape((2, 2, SUB, BLK, HD), bf16)
     return pl.pallas_call(
         pack_kernel,
-        out_shape=(both, both, one, one, one, one, shape((n, BLK + EXTRA, 2 * HD), bf16)),
-        in_specs=[SMEM] + [VMEM] * 5,
-        out_specs=(VMEM,) * 7,
-        compiler_params=params(24),
-        cost_estimate=pl.CostEstimate(flops=0, bytes_accessed=6 << 20, transcendentals=0),
+        out_shape=(both, both, one, one, one, one),
+        in_specs=[SMEM] + [HBM] * 2,
+        out_specs=(HBM,) * 6,
+        scratch_shapes=[pltpu.SemaphoreType.DMA((2 * HQ,))],
+        compiler_params=params(4),
+        cost_estimate=pl.CostEstimate(flops=0, bytes_accessed=4 << 20, transcendentals=0),
         name="pack",
-    )(place, query, grad_out, keys, values, positions)
-
-
-def attend_kernel(
-    blocks_ref, own_ref, x_ref, za_ref, da_ref, zb_ref, db_ref, kv_hbm, table_ref, ks_ref, qs_ref,
-    go_ref, gx_ref, gza_ref, gda_ref, gzb_ref, gdb_ref, term_ref, dkv_ref,
-    s_scr, p_scr, qd_scr, kv_ref, cs_ref, kr_ref, kt_ref, q_scr, qt_scr, dt_scr, dq_scr, m_scr, l_scr, e_scr,
-    gq_scr, dk_ref, dv_ref, tq_ref, sems, kv_sem,
-):
+    )(place, query, grad_out)
+
+
+def prep_kernel(kv_ref, table_ref, ks_ref, cs_ref, kr_ref, kt_ref):
     n = kv_ref.shape[0]
-    kv_copy = pltpu.make_async_copy(kv_hbm, kv_ref, kv_sem)
-    kv_copy.start()
-    first, second = pl.ds(0, SUB), pl.ds(SUB, SUB)
-    copies = [
-        pltpu.make_async_copy(src, qd_scr.at[u, :, heads], sems.at[i])
-        for i, (src, u, heads) in enumerate((
-            (own_ref.at[0], 0, first), (own_ref.at[1], 0, second),
-            (x_ref.at[0], 1, first), (x_ref.at[1], 1, second),
-            (za_ref, 2, first), (zb_ref, 2, second),
-            (da_ref, 3, first), (db_ref, 3, second),
-        ))
-    ]
-    for copy in copies:
-        copy.start()
-    dk_ref[...] = jnp.zeros_like(dk_ref)
-    dv_ref[...] = jnp.zeros_like(dv_ref)
-    tq_ref[...] = jnp.zeros_like(tq_ref)
     sign = jnp.where(lax.broadcasted_iota(jnp.int32, (BLK, HD), 1) < HD // 2, -1.0, 1.0)
     row = lax.broadcasted_iota(jnp.int32, (BLK, BLK), 0).astype(f32)
-    kv_copy.wait()
 
     def pick(i, part):
         pos = kv_ref[i, BLK : BLK + EXTRA, part * HD : (part + 1) * HD].astype(f32)[:1]
@@ -165,14 +177,70 @@
         return carry
 
     lax.fori_loop(0, n // per, ready, 0)
-    for copy in copies:
-        copy.wait()
+
+
+def prep(kv, table, ks):
+    length = kv.shape[0] * BLK
+    return pl.pallas_call(
+        prep_kernel,
+        out_shape=(
+            shape((length, 2 * HD), f32),
+            shape((length, HD), bf16),
+            shape((length // KEYS, HD, KEYS), bf16),
+        ),
+        in_specs=[VMEM] * 3,
+        out_specs=(VMEM,) * 3,
+        compiler_params=params(12),
+        cost_estimate=pl.CostEstimate(flops=1 << 29, bytes_accessed=5 << 20, transcendentals=0),
+        name="prep",
+    )(kv, table, ks)
+
+
+def attend_kernel(stage, blocks_ref, *refs):
+    take = iter(refs)
+    get = lambda count: [next(take) for _ in range(count)]
+    parts = get(2 if stage == 0 else 4)
+    kv_hbm, cs_hbm, kr_hbm, kt_hbm, qs_ref = get(5)
+    dk_in, dv_in, tq_in = get(3) if stage else (None,) * 3
+    grads = get(2 if stage == 0 else 4)
+    last = get(3 if stage == 0 else 2)
+    s_scr, p_scr, qd_scr, kv_ref, cs_ref, kr_ref, kt_ref, q_scr, dq_scr, m_scr, e_scr, gq_scr, dk_ref, dv_ref = get(14)
+    tq_ref, sems, kv_sems = get(3)
+    n = kv_ref.shape[0]
+    first, second = pl.ds(0, SUB), pl.ds(SUB, SUB)
+    if stage == 0:
+        places = lambda r: ((r[0].at[0], 0, first), (r[0].at[1], 0, second), (r[1].at[0], 1, first), (r[1].at[1], 1, second))
+    else:
+        places = lambda r: ((r[0], 0, first), (r[2], 0, second), (r[1], 1, first), (r[3], 1, second))
+    pieces = [(src, qd_scr.at[u, :, heads]) for src, u, heads in places(parts)]
+    pieces += [(kr_hbm, kr_ref), (kv_hbm, kv_ref), (cs_hbm, cs_ref), (kt_hbm, kt_ref)]
+    if stage:
+        pieces += [(dk_in, dk_ref), (dv_in, dv_ref)]
+    copies = [pltpu.make_async_copy(src, dst, kv_sems.at[i]) for i, (src, dst) in enumerate(pieces)]
+    for copy in copies:
+        copy.start()
+    if stage == 0:
+        dk_ref[...] = jnp.zeros_like(dk_ref)
+        dv_ref[...] = jnp.zeros_like(dv_ref)
+        tq_ref[...] = jnp.zeros_like(tq_ref)
+    else:
+        tq_ref[...] = tq_in[...]
+    rows, (kr_copy, kv_copy, cs_copy, kt_copy), sums = copies[:4], copies[4:8], copies[8:]
+    per = KEYS // BLK
+
+    def wait(u, *which):
+        @pl.when(u == 0)
+        def _():
+            for copy in which:
+                copy.wait()
+
     sub8 = lax.broadcasted_iota(jnp.int32, (8, ROWS), 0)
     lane = lax.broadcasted_iota(jnp.int32, (8, ROWS), 1)
     group = lax.broadcasted_iota(jnp.int32, (CHUNK // 8, 8, ROWS), 0) * 8
 
     def unit(u, carry):
         b0, b1 = blocks_ref[2 * u], blocks_ref[2 * u + 1]
+        wait(u, *rows, cs_copy)
         tabs = []
         for b in (b0, b1):
             toks = pl.ds(pl.multiple_of(b * BLK, BLK), BLK)
@@ -181,39 +249,45 @@
             cols = slice(h * BLK, (h + 1) * BLK)
             r = turn(qd_scr[u, 0, h].astype(f32) * qs_ref[h : h + 1, :], *tabs[h // SUB])
             q_scr[cols, :] = r.astype(bf16)
-            qt_scr[:, cols] = r.T.astype(bf16)
-            dt_scr[:, cols] = qd_scr[u, 1, h].astype(f32).T.astype(bf16)
         dq_scr[...] = jnp.zeros_like(dq_scr)
         token = jnp.where(lane < ROWS // 2, b0, b1) * BLK + (lane & (BLK - 1)) - sub8
         steps = jnp.maximum(b0, b1) // per + 1
 
-        def look(w, stats):
+        wait(u, kr_copy, kv_copy)
+
+        def look(w, stats, masked):
             m, l, d = stats
             for j in range(KEYS // CHUNK):
                 at = pl.ds(pl.multiple_of(w * KEYS + j * CHUNK, CHUNK), CHUNK)
                 vals = kv_ref[pl.ds(w * per + j * (CHUNK // BLK), CHUNK // BLK), :BLK, HD:]
-                s = jnp.dot(kr_ref[at, :], qt_scr[...], preferred_element_type=f32)
-                dp = jnp.dot(vals.reshape(CHUNK, HD), dt_scr[...], preferred_element_type=f32)
+                s = dot_t(kr_ref[at, :], q_scr[...]) * EXP2
+                dp = dot_t(vals.reshape(CHUNK, HD), qd_scr[u, 1].reshape(ROWS, HD))
                 p_scr[at, :] = dp
                 s3 = s.reshape(CHUNK // 8, 8, ROWS)
                 dp3 = dp.reshape(CHUNK // 8, 8, ROWS)
-                s3 = jnp.where(group <= (token - (w * KEYS + j * CHUNK))[None], s3, NEG)
+                if masked:
+                    s3 = jnp.where(group <= (token - (w * KEYS + j * CHUNK))[None], s3, NEG)
                 s_scr[at, :] = s3.reshape(CHUNK, ROWS)
                 mn = jnp.maximum(m, jnp.max(s3, axis=0))
-                a = jnp.exp2((m - mn) * EXP2)
-                e = jnp.exp2((s3 - mn[None]) * EXP2)
+                a = jnp.exp2(m - mn)
+                e = jnp.exp2(s3 - mn[None])
                 m, l, d = mn, l * a + jnp.sum(e, axis=0), d * a + jnp.sum(e * dp3, axis=0)
             return m, l, d
 
         zero = jnp.zeros((8, ROWS), f32)
-        m, l, d = lax.fori_loop(0, steps, look, (zero + NEG, zero, zero))
+        stats = (zero + NEG, zero, zero)
+        clear = jnp.minimum(b0, b1) // per
+        stats = lax.fori_loop(0, clear, lambda w, c: look(w, c, False), stats)
+        m, l, d = lax.fori_loop(clear, steps, lambda w, c: look(w, c, True), stats)
         top = jnp.max(m, axis=0, keepdims=True)
-        w = jnp.exp2((m - top) * EXP2)
+        w = jnp.exp2(m - top)
         total = jnp.sum(l * w, axis=0, keepdims=True)
         delta = jnp.sum(d * w, axis=0, keepdims=True) / total
-        shift = top * EXP2 + jnp.log2(total)
+        shift = top + jnp.log2(total)
         m_scr[...] = jnp.broadcast_to(shift, m_scr.shape)
         e_scr[...] = jnp.broadcast_to(delta, e_scr.shape)
+
+        wait(u, kt_copy, *sums)
 
         def back(w, carry):
             shift, delta = m_scr[...][None], e_scr[...][None]
@@ -222,7 +296,7 @@
                 at = pl.ds(pl.multiple_of(w * KEYS + j * CHUNK, CHUNK), CHUNK)
                 s3 = s_scr[at, :].reshape(CHUNK // 8, 8, ROWS)
                 dp3 = p_scr[at, :].reshape(CHUNK // 8, 8, ROWS)
-                p = jnp.exp2(s3 * EXP2 - shift)
+                p = jnp.exp2(s3 - shift)
                 ds = (p * (dp3 - delta)).reshape(CHUNK, ROWS).astype(bf16)
                 p = p.reshape(CHUNK, ROWS).astype(bf16)
                 dv_ref[at, :] += jnp.dot(p, qd_scr[u, 1].reshape(ROWS, HD), preferred_element_type=f32)
@@ -243,18 +317,19 @@
             tq_ref[h : h + 1, :] += jnp.sum(g * qd_scr[u, 0, h].astype(f32), axis=0, keepdims=True)
         return carry
 
-    lax.fori_loop(0, 4, unit, 0)
-    copies = [
-        pltpu.make_async_copy(gq_scr.at[u, heads], dst, sems.at[i])
-        for i, (dst, u, heads) in enumerate((
-            (go_ref.at[0], 0, first), (go_ref.at[1], 0, second),
-            (gx_ref.at[0], 1, first), (gx_ref.at[1], 1, second),
-            (gza_ref, 2, first), (gzb_ref, 2, second),
-            (gda_ref, 3, first), (gdb_ref, 3, second),
-        ))
-    ]
+    lax.fori_loop(0, 2, unit, 0)
+    outs = [(gq_scr.at[u, heads], dst) for dst, u, heads in places(grads)]
+    if stage == 0:
+        outs += [(dk_ref, last[0]), (dv_ref, last[1])]
+    copies = [pltpu.make_async_copy(src, dst, sems.at[i]) for i, (src, dst) in enumerate(outs)]
     for copy in copies:
         copy.start()
+    if stage == 0:
+        last[2][...] = tq_ref[...]
+        for copy in copies:
+            copy.wait()
+        return
+    term_ref, dkv_ref = last
 
     def finish(c, tk):
         at = pl.ds(pl.multiple_of(c * BLK, BLK), BLK)
@@ -265,7 +340,7 @@
         g = unturn(g, cs_ref[at, :HD], cs_ref[at, HD:])
         return tk + jnp.sum(g * kv_ref[c, :BLK, :HD].astype(f32), axis=0, keepdims=True)
 
-    tk = lax.fori_loop(0, n, finish, jnp.zeros((1, HD), f32))
+    tk = lax.fori_loop(0, n, finish, jnp.zeros((1, HD), f32), unroll=4)
     terms = jnp.concatenate([tq_ref[...], jnp.broadcast_to(tk, (8, HD))], axis=0)
     for j in range(term_ref.shape[0]):
         term_ref[j] = terms
@@ -273,46 +348,46 @@
         copy.wait()
 
 
-def attend(blocks, parts, kv, table, ks, qs, copies_of_term):
+def attend(stage, blocks, parts, kv, cs, kr, kt, qs, before, sequences):
     n = kv.shape[0]
     length = n * BLK
     one, both = shape((SUB, BLK, HD), bf16), shape((2, SUB, BLK, HD), bf16)
-    pairs = 4 * ROWS * length // 2
-    return pl.pallas_call(
-        attend_kernel,
-        out_shape=(
-            both, both, one, one, one, one,
-            shape((copies_of_term, 2 * SUB + 8, HD), f32),
-            shape(kv.shape, bf16),
-        ),
-        in_specs=[SMEM] + [ANY] * 7 + [VMEM] * 3,
-        out_specs=(ANY,) * 6 + (VMEM,) * 2,
+    total = shape((length, HD), f32)
+    pairs = 2 * ROWS * length // 2
+    if stage == 0:
+        out_shape = (both, both, total, total, shape((2 * SUB, HD), f32))
+        out_specs = (HBM,) * 2 + (ANY,) * 2 + (VMEM,)
+    else:
+        out_shape = (one,) * 4 + (shape((sequences, 2 * SUB + 8, HD), f32), shape(kv.shape, bf16))
+        out_specs = (HBM,) * 4 + (VMEM,) * 2
+    return pl.pallas_call(
+        lambda *refs: attend_kernel(stage, *refs),
+        out_shape=out_shape,
+        in_specs=[SMEM] + [ANY] * (len(parts) + 4) + [VMEM] + ([ANY, ANY, VMEM] if stage else []),
+        out_specs=out_specs,
         scratch_shapes=[
             pltpu.VMEM((length, ROWS), f32),
             pltpu.VMEM((length, ROWS), f32),
-            pltpu.VMEM((4, 2, 2 * SUB, BLK, HD), bf16),
+            pltpu.VMEM((2, 2, 2 * SUB, BLK, HD), bf16),
             pltpu.VMEM(kv.shape, bf16),
             pltpu.VMEM((length, 2 * HD), f32),
             pltpu.VMEM((length, HD), bf16),
             pltpu.VMEM((length // KEYS, HD, KEYS), bf16),
             pltpu.VMEM((ROWS, HD), bf16),
-            pltpu.VMEM((HD, ROWS), bf16),
-            pltpu.VMEM((HD, ROWS), bf16),
             pltpu.VMEM((HD, ROWS), f32),
             pltpu.VMEM((8, ROWS), f32),
             pltpu.VMEM((8, ROWS), f32),
-            pltpu.VMEM((8, ROWS), f32),
-            pltpu.VMEM((4, 2 * SUB, BLK, HD), bf16),
+            pltpu.VMEM((2, 2 * SUB, BLK, HD), bf16),
             pltpu.VMEM((length, HD), f32),
             pltpu.VMEM((length, HD), f32),
             pltpu.VMEM((2 * SUB, HD), f32),
-            pltpu.SemaphoreType.DMA((8,)),
-            pltpu.SemaphoreType.DMA,
+            pltpu.SemaphoreType.DMA((6,)),
+            pltpu.SemaphoreType.DMA((10,)),
         ],
-        compiler_params=params(44),
+        compiler_params=params(36),
         cost_estimate=pl.CostEstimate(flops=pairs * HD * 20, bytes_accessed=8 << 20, transcendentals=pairs * 2),
         name="attend",
-    )(blocks, *parts, kv, table, ks, qs)
+    )(blocks, *parts, kv, cs, kr, kt, qs, *before)
 
 
 def add_kernel(term_ref, dkv_in, dkv_ref, pair, sems):
@@ -426,26 +501,22 @@
     def send(a, flip, step):
         return lax.ppermute(a, "seq", pairs(flip, step))
 
-    own, to_x, to_za, to_da, to_zb, to_db, kv = pack(
-        place, query[0], grad_out[0], keys[0], values[0], positions, n
-    )
-    kv = lax.all_to_all(kv, "seq", 0, 0, tiled=True)
+    kv = lax.all_to_all(pack_kv(keys[0], values[0], positions, n), "seq", 0, 0, tiled=True)
+    own, to_x, to_za, to_da, to_zb, to_db = pack(place, query[0], grad_out[0])
     in_x = send(to_x, 1, 0)
     in_za, in_da = send(to_za, 0, 1), send(to_da, 1, 1)
     in_zb, in_db = send(to_zb, 0, -1), send(to_db, 1, -1)
 
     q_gain = lax.dynamic_slice_in_dim(q_scale.reshape(HK, 2 * SUB, HD), kind, 1, 0)[0]
     k_gain = lax.dynamic_slice_in_dim(k_scale.reshape(HK, HD), kind, 1, 0)
+    keys_side = (kv, *prep(kv, angle_tables(), k_gain))
+    sequences = lax.axis_size("dp")
+    blocks = jnp.stack([me, me, me ^ half, me ^ half]).astype(jnp.int32)
+    go, gx, *sums = attend(0, blocks, (own, in_x), *keys_side, q_gain, (), sequences)
     pair = lambda side: [side * half + za, side * half + zb]
-    blocks = jnp.stack([me, me, me ^ half, me ^ half, *pair(x), *pair(1 - x)]).astype(jnp.int32)
-    go, gx, gza, gda, gzb, gdb, term, dkv = attend(
-        blocks,
-        (own, in_x, in_za, in_da, in_zb, in_db),
-        kv,
-        angle_tables(),
-        k_gain,
-        q_gain,
-        lax.axis_size("dp"),
+    blocks = jnp.stack(pair(x) + pair(1 - x)).astype(jnp.int32)
+    gza, gda, gzb, gdb, term, dkv = attend(
+        1, blocks, (in_za, in_da, in_zb, in_db), *keys_side, q_gain, sums, sequences
     )
 
     term = lax.all_to_all(term, "dp", 0, 0, tiled=True)

time: 165 us -> 141 us (0.85)
  waiting for transfers between devices: 55.8 us -> 39.8 us
  local copies, waits for them, and re-layouts: 7.97 us -> 1.54 us
  starting transfers between devices: 63.4 us -> 60.1 us
    ppermute x10, waiting for transfers between devices: 30.6 us -> 6.5 us  [send(): return lax.ppermute(a, 'seq', pairs(flip, step))]
    all_to_all x1, waiting for transfers between devices: 0.01 us -> 8.22 us  [shards(): lax.all_to_all(pack_kv(keys[0], values[0], positions, n), 'seq', 0, 0, ti...]
    unnamed x24 -> x18, local copies, waits for them, and re-layouts: 7.88 us -> 1.52 us
    ppermute x10, starting transfers between devices: 33.1 us -> 31.4 us  [send(): return lax.ppermute(a, 'seq', pairs(flip, step))]
    pallas_call x2 -> x5, Pallas kernels: 30.7 us -> 32.1 us  [the longest x2 25.4 us: attend(): pl.pallas_call(lambda *refs: attend_kernel(stage, *refs), out_shape=out_s...]
  transfers between devices with their start and end apart: 13 -> 13, of which waited for: 5 -> 4; matrix products, arithmetic and copies ran while one was open for 1% -> 1% of each run, Pallas kernels for 2% -> 12%
where the time goes in v2:
time: 141 us; the launch traced here: 140 us
  starting transfers between devices  60.1 us (43%)
  waiting for transfers between devices  39.8 us (28%)
  Pallas kernels  35.7 us (25%)
  local copies, waits for them, and re-layouts  1.54 us (1%)
    ppermute x10, starting transfers between devices, send(): return lax.ppermute(a, 'seq', pairs(flip, step))  31.4 us
    pallas_call x2, Pallas kernels, attend(): pl.pallas_call(lambda *refs: attend_kernel(stage, *refs), out_shape=out_s...  25.4 us
    all_to_all x1, waiting for transfers between devices, shards(): dkv = lax.all_to_all(dkv, 'seq', 0, 0, tiled=True)  25.1 us
    all_to_all x1, starting transfers between devices, shards(): term = lax.all_to_all(term, 'dp', 0, 0, tiled=True)  12.2 us
    all_to_all x1, starting transfers between devices, shards(): lax.all_to_all(pack_kv(keys[0], values[0], positions, n), 'seq', 0, 0, ti...  12 us
    all_to_all x1, waiting for transfers between devices, shards(): lax.all_to_all(pack_kv(keys[0], values[0], positions, n), 'seq', 0, 0, ti...  8.22 us
    ppermute x10, waiting for transfers between devices, send(): return lax.ppermute(a, 'seq', pairs(flip, step))  6.5 us
    all_to_all x1, starting transfers between devices, shards(): dkv = lax.all_to_all(dkv, 'seq', 0, 0, tiled=True)  4.45 us
  transfers between devices with their start and end apart: 13, of which 4 were waited for; matrix products, arithmetic and copies ran while one was open for 1% of the time, Pallas kernels for 12%

profile of v2, /device:TPU:1, one launch (start us, length us, event | category | flops | bytes accessed | tf_op | source)
XLA Modules:
  0.0 139.5 jit_solution(4455591665774923133)
XLA Ops:
  0.6 2.2 %pack_kv.1 = bf16[16,144,256]{2,1,0:T(8,128)(2,1)} custom-call(bf16[128,512]{1,0:T(8,128)(2,1)} %bitcast.36, bf16[128,512]{1,0:T(8,128)(2,1)} %bitcast.37, s32[1,128]{1,0:T(1,128)} %pos_hbm.1), custom_call_target="tpu_custom_call" | custom-call | bytes 2097152 | tf_op jit(solution)/shard_map/pack_kv/pallas_call | solution.py:99
  2.8 12.0 %all-to-all-start = ((bf16[16,144,256]{2,1,0:T(8,128)(2,1)}), bf16[16,144,256]{2,1,0:T(8,128)(2,1)S(1)}, u32[]{:S(2)}, u32[]{:S(2)}) async-start(bf16[16,144,256]{2,1,0:T(8,128)(2,1)} %pack_kv.1), calls=%async_computation | async-start | bytes 2359296 | tf_op jit(solution)/shard_map/all_to_all | solution.py:504
  15.0 2.3 %pack.1 = (bf16[2,2,4,128,128]{4,3,2,1,0:T(8,128)(2,1)S(1)}, bf16[2,2,4,128,128]{4,3,2,1,0:T(8,128)(2,1)}, bf16[2,4,128,128]{3,2,1,0:T(8,128)(2,1)}, bf16[2,4,12...) custom-call(s32[2]{0:T(128)S(1)} %pad_add_fusion.place_ref, ...), custom_call_target="tpu_custom_call" | custom-call | bytes 4194304 | tf_op jit(solution)/shard_map/pack/pallas_call | solution.py:138
  18.1 3.3 %collective-permute-start.4 = (bf16[2,2,4,128,128]{4,3,2,1,0:T(8,128)(2,1)}, bf16[2,2,4,128,128]{4,3,2,1,0:T(8,128)(2,1)S(1)}, u32[]{:S(2)}, u32[]{:S(2)}) collective-permute-start(bf16[2,2,4,128,128]{4,3,2,1,0:T(8,128)(2,1)} %get-tuple-element.44), channel_id=1, source_target_pairs={{0,8},{1,9},{2,10},{3,11},{4,12},{5,13},{6,14},{7,15},{8,0},{9,1},... | collective-permute-start | bytes 1572872 | tf_op jit(solution)/shard_map/ppermute | solution.py:502
  21.3 3.1 %collective-permute-start = (bf16[2,4,128,128]{3,2,1,0:T(8,128)(2,1)}, bf16[2,4,128,128]{3,2,1,0:T(8,128)(2,1)S(1)}, u32[]{:S(2)}, u32[]{:S(2)}) collective-permute-start(bf16[2,4,128,128]{3,2,1,0:T(8,128)(2,1)} %get-tuple-element.36), channel_id=1, source_target_pairs={{0,1},{1,0},{2,3},{3,2},{4,5},{5,4},{6,7},{7,6},{8,9},{9,8},{10,11... | collective-permute-start | bytes 786440 | tf_op jit(solution)/shard_map/ppermute | solution.py:502
  24.4 2.0 %collective-permute-start.1 = (bf16[2,4,128,128]{3,2,1,0:T(8,128)(2,1)}, bf16[2,4,128,128]{3,2,1,0:T(8,128)(2,1)S(1)}, u32[]{:S(2)}, u32[]{:S(2)}) collective-permute-start(bf16[2,4,128,128]{3,2,1,0:T(8,128)(2,1)} %get-tuple-element.37), channel_id=1, source_target_pairs={{0,9},{1,8},{2,11},{3,10},{4,13},{5,12},{6,15},{7,14},{8,1},{9,0},... | collective-permute-start | bytes 786440 | tf_op jit(solution)/shard_map/ppermute | solution.py:502
  26.5 4.5 %collective-permute-start.2 = (bf16[2,4,128,128]{3,2,1,0:T(8,128)(2,1)}, bf16[2,4,128,128]{3,2,1,0:T(8,128)(2,1)}, u32[]{:S(2)}, u32[]{:S(2)}) collective-permute-start(bf16[2,4,128,128]{3,2,1,0:T(8,128)(2,1)} %get-tuple-element.38), channel_id=1, source_target_pairs={{0,7},{1,2},{2,1},{3,4},{4,3},{5,6},{6,5},{7,0},{8,15},{9,10},{10,... | collective-permute-start | bytes 786440 | tf_op jit(solution)/shard_map/ppermute | solution.py:502
  30.9 3.1 %collective-permute-start.3 = (bf16[2,4,128,128]{3,2,1,0:T(8,128)(2,1)}, bf16[2,4,128,128]{3,2,1,0:T(8,128)(2,1)}, u32[]{:S(2)}, u32[]{:S(2)}) collective-permute-start(bf16[2,4,128,128]{3,2,1,0:T(8,128)(2,1)} %get-tuple-element.39), channel_id=1, source_target_pairs={{0,15},{1,10},{2,9},{3,12},{4,11},{5,14},{6,13},{7,8},{8,7},{9,2},... | collective-permute-start | bytes 786440 | tf_op jit(solution)/shard_map/ppermute | solution.py:502
  35.0 8.2 %all-to-all-done.kv_ref.refs_3_.refs_5_ = bf16[16,144,256]{2,1,0:T(8,128)(2,1)S(1)} async-done(((bf16[16,144,256]{2,1,0:T(8,128)(2,1)}), bf16[16,144,256]{2,1,0:T(8,128)(2,1)S(1)}, u32[]{:S(2)}, u32[]{:S(2)}) %all-to-all-start) | async-done | bytes 1179680 | tf_op jit(solution)/shard_map/all_to_all | solution.py:504
  43.2 2.3 %prep.1 = (f32[2048,256]{1,0:T(8,128)S(1)}, bf16[2048,128]{1,0:T(8,128)(2,1)S(1)}, bf16[4,128,512]{2,1,0:T(8,128)(2,1)S(1)}) custom-call(bf16[16,144,256]{2,1,0:T(8,128)(2,1)S(1)} %all-to-all-done.kv_ref.refs_3_.refs_5_, bf16[2,128,512]{2,1,0:T(8,128)(2,1)S(1)} %maximum_maximum_fusion.table_ref, f32[1,128]{1,0:T(1,128)S(1)} %constant_dynamic-slice_fusion.ks_ref), custom_call_target="tpu_custom_call" | custom-call | flops 536870912 | bytes 5242880 | tf_op jit(solution)/shard_map/prep/pallas_call | solution.py:184
  45.5 10.2 %attend.2 = (bf16[2,4,128,128]{3,2,1,0:T(8,128)(2,1)S(1)}, bf16[2,4,128,128]{3,2,1,0:T(8,128)(2,1)S(1)}, f32[2048,128]{1,0:T(8,128)S(1)}, f32[2048,128]{1,0:T(8,128)S(1)}, f32[8,128]{1,0:T(8,128)S(1)}) custom-call(s32[4]{0:T(128)S(1)} %pad_add_fusion.2.refs_0_, bf16[2,2,4,128,128]{4,3,2,1,0:T(8,128)(2,1)S(1)} %copy-done.5, ...), custom_call_target="tpu_custom_call" | custom-call | flops 5368709120 | bytes 8388608 | tf_op jit(solution)/shard_map/attend/pallas_call | solution.py:363
  56.5 1.5 %collective-permute-done.1.refs_2_ = bf16[2,4,128,128]{3,2,1,0:T(8,128)(2,1)S(1)} collective-permute-done((bf16[2,4,128,128]{3,2,1,0:T(8,128)(2,1)}, bf16[2,4,128,128]{3,2,1,0:T(8,128)(2,1)S(1)}, u32[]{:S(2)}, u32[]{:S(2)}) %collective-permute-start.1) | collective-permute-done | bytes 262176 | tf_op jit(solution)/shard_map/ppermute | solution.py:502
  58.0 15.2 %attend.3 = (bf16[4,128,128]{2,1,0:T(8,128)(2,1)}, bf16[4,128,128]{2,1,0:T(8,128)(2,1)}, bf16[4,128,128]{2,1,0:T(8,128)(2,1)S(1)}, bf16[4,128,128]{2,1,0:T(8,128...) custom-call(s32[4]{0:T(128)S(1)} %pad_add_fusion.1.refs_0_, ...), custom_call_target="tpu_custom_call" | custom-call | flops 5368709120 | bytes 8388608 | tf_op jit(solution)/shard_map/attend/pallas_call | solution.py:363
  73.2 12.2 %all-to-all-start.1 = ((f32[32,16,128]{2,1,0:T(8,128)}), f32[32,16,128]{2,1,0:T(8,128)S(1)}, u32[]{:S(2)}, u32[]{:S(2)}) async-start(f32[32,16,128]{2,1,0:T(8,128)} %get-tuple-element.48), calls=%async_computation.1 | async-start | bytes 524288 | tf_op jit(solution)/shard_map/all_to_all | solution.py:522
  85.4 1.9 %collective-permute-start.5 = (bf16[2,4,128,128]{3,2,1,0:T(8,128)(2,1)S(1)}, bf16[2,4,128,128]{3,2,1,0:T(8,128)(2,1)S(1)}, u32[]{:S(2)}, u32[]{:S(2)}) collective-permute-start(bf16[2,4,128,128]{3,2,1,0:T(8,128)(2,1)S(1)} %copy-done.7), channel_id=1, source_target_pairs={{0,8},{1,9},{2,10},{3,11},{4,12},{5,13},{6,14},{7,15},{8,0},{9,1},... | collective-permute-start | bytes 786440 | tf_op jit(solution)/shard_map/ppermute | solution.py:502
  87.3 1.9 %collective-permute-start.6 = (bf16[4,128,128]{2,1,0:T(8,128)(2,1)}, bf16[4,128,128]{2,1,0:T(8,128)(2,1)S(1)}, u32[]{:S(2)}, u32[]{:S(2)}) collective-permute-start(bf16[4,128,128]{2,1,0:T(8,128)(2,1)} %get-tuple-element.52), channel_id=1, source_target_pairs={{0,1},{1,0},{2,3},{3,2},{4,5},{5,4},{6,7},{7,6},{8,9},{9,8},{10,11... | collective-permute-start | bytes 393224 | tf_op jit(solution)/shard_map/ppermute | solution.py:502
  89.3 4.5 %collective-permute-start.7 = (bf16[4,128,128]{2,1,0:T(8,128)(2,1)}, bf16[4,128,128]{2,1,0:T(8,128)(2,1)S(1)}, u32[]{:S(2)}, u32[]{:S(2)}) collective-permute-start(bf16[4,128,128]{2,1,0:T(8,128)(2,1)} %get-tuple-element.53), channel_id=1, source_target_pairs={{0,9},{1,8},{2,11},{3,10},{4,13},{5,12},{6,15},{7,14},{8,1},{9,0},... | collective-permute-start | bytes 393224 | tf_op jit(solution)/shard_map/ppermute | solution.py:502
  93.8 5.2 %collective-permute-start.8 = (bf16[4,128,128]{2,1,0:T(8,128)(2,1)S(1)}, bf16[4,128,128]{2,1,0:T(8,128)(2,1)S(1)}, u32[]{:S(2)}, u32[]{:S(2)}) collective-permute-start(bf16[4,128,128]{2,1,0:T(8,128)(2,1)S(1)} %get-tuple-element.54), channel_id=1, source_target_pairs={{0,7},{1,2},{2,1},{3,4},{4,3},{5,6},{6,5},{7,0},{8,15},{9,10},{10,... | collective-permute-start | bytes 393224 | tf_op jit(solution)/shard_map/ppermute | solution.py:502
  99.0 1.9 %collective-permute-start.9 = (bf16[4,128,128]{2,1,0:T(8,128)(2,1)S(1)}, bf16[4,128,128]{2,1,0:T(8,128)(2,1)S(1)}, u32[]{:S(2)}, u32[]{:S(2)}) collective-permute-start(bf16[4,128,128]{2,1,0:T(8,128)(2,1)S(1)} %get-tuple-element.55), channel_id=1, source_target_pairs={{0,15},{1,10},{2,9},{3,12},{4,11},{5,14},{6,13},{7,8},{8,7},{9,2},... | collective-permute-start | bytes 393224 | tf_op jit(solution)/shard_map/ppermute | solution.py:502
  101.9 5.0 %collective-permute-done.9.db_ref = bf16[4,128,128]{2,1,0:T(8,128)(2,1)S(1)} collective-permute-done((bf16[4,128,128]{2,1,0:T(8,128)(2,1)S(1)}, bf16[4,128,128]{2,1,0:T(8,128)(2,1)S(1)}, u32[]{:S(2)}, u32[]{:S(2)}) %collective-permute-start.9) | collective-permute-done | bytes 131104 | tf_op jit(solution)/shard_map/ppermute | solution.py:502
  106.8 4.5 %all-to-all-start.2 = ((bf16[16,144,256]{2,1,0:T(8,128)(2,1)}), bf16[16,144,256]{2,1,0:T(8,128)(2,1)S(1)}, u32[]{:S(2)}, u32[]{:S(2)}) async-start(bf16[16,144,256]{2,1,0:T(8,128)(2,1)} %add.63), calls=%async_computation.2 | async-start | bytes 2359296 | tf_op jit(solution)/shard_map/all_to_all | solution.py:525
  111.8 1.8 %unpack.1 = bf16[128,4096]{1,0:T(8,128)(2,1)} custom-call(s32[2]{0:T(128)S(1)} %pad_add_fusion.place_ref, bf16[2,4,128,128]{3,2,1,0:T(8,128)(2,1)S(1)} %get-tuple-element.56.own_ref, bf16[2,4,128,128]{3,2,1,0:T(8,128)(2,1)S(1)} %collective-permute-done.5.x_ref, bf16[4,128,128]{2,1,0:T(8,128)(2,1)S(1)} %collective-permute-done.6.za_ref, ...), custom_call_target="tpu_custom_call" | custom-call | bytes 2097152 | tf_op jit(solution)/shard_map/unpack/pallas_call | solution.py:439
  113.5 25.1 %all-to-all-done.2.dkv_ref = bf16[16,144,256]{2,1,0:T(8,128)(2,1)S(1)} async-done(((bf16[16,144,256]{2,1,0:T(8,128)(2,1)}), bf16[16,144,256]{2,1,0:T(8,128)(2,1)S(1)}, u32[]{:S(2)}, u32[]{:S(2)}) %all-to-all-start.2) | async-done | bytes 1179680 | tf_op jit(solution)/shard_map/all_to_all | solution.py:525
  138.6 0.9 final.1
  (42 shorter events, 3.8 us)
Async XLA Ops:
  0.6 33.7 %copy-start = (f32[4096]{0:T(1024)S(1)}, f32[4096]{0:T(1024)}, u32[]{:S(2)}) copy-start(f32[4096]{0:T(1024)} %param.12) | copy-start | bytes 49156
  2.8 12.2 %copy-start.1 = (bf16[1,128,4096]{2,1,0:T(8,128)(2,1)S(1)}, bf16[1,128,4096]{2,1,0:T(8,128)(2,1)}, u32[]{:S(2)}) copy-start(bf16[1,128,4096]{2,1,0:T(8,128)(2,1)} %param.7) | copy-start | bytes 3145732
  2.8 12.2 %copy-start.2 = (bf16[1,128,4096]{2,1,0:T(8,128)(2,1)S(1)}, bf16[1,128,4096]{2,1,0:T(8,128)(2,1)}, u32[]{:S(2)}) copy-start(bf16[1,128,4096]{2,1,0:T(8,128)(2,1)} %param.10) | copy-start | bytes 3145732
  2.8 40.4 %all-to-all-start = ((bf16[16,144,256]{2,1,0:T(8,128)(2,1)}), bf16[16,144,256]{2,1,0:T(8,128)(2,1)S(1)}, u32[]{:S(2)}, u32[]{:S(2)}) async-start(bf16[16,144,256]{2,1,0:T(8,128)(2,1)} %pack_kv.1), calls=%async_computation | async-start | bytes 2359296 | tf_op jit(solution)/shard_map/all_to_all | solution.py:504
  14.9 19.4 %copy-start.3 = (f32[512]{0:T(512)S(1)}, f32[512]{0:T(512)}, u32[]{:S(2)}) copy-start(f32[512]{0:T(512)} %param.13) | copy-start | bytes 6148
  17.3 0.8 copy-start.4
  18.1 27.4 %collective-permute-start.4 = (bf16[2,2,4,128,128]{4,3,2,1,0:T(8,128)(2,1)}, bf16[2,2,4,128,128]{4,3,2,1,0:T(8,128)(2,1)S(1)}, u32[]{:S(2)}, u32[]{:S(2)}) collective-permute-start(bf16[2,2,4,128,128]{4,3,2,1,0:T(8,128)(2,1)} %get-tuple-element.44), channel_id=1, source_target_pairs={{0,8},{1,9},{2,10},{3,11},{4,12},{5,13},{6,14},{7,15},{8,0},{9,1},... | collective-permute-start | bytes 1572872 | tf_op jit(solution)/shard_map/ppermute | solution.py:502
  21.3 35.1 %collective-permute-start = (bf16[2,4,128,128]{3,2,1,0:T(8,128)(2,1)}, bf16[2,4,128,128]{3,2,1,0:T(8,128)(2,1)S(1)}, u32[]{:S(2)}, u32[]{:S(2)}) collective-permute-start(bf16[2,4,128,128]{3,2,1,0:T(8,128)(2,1)} %get-tuple-element.36), channel_id=1, source_target_pairs={{0,1},{1,0},{2,3},{3,2},{4,5},{5,4},{6,7},{7,6},{8,9},{9,8},{10,11... | collective-permute-start | bytes 786440 | tf_op jit(solution)/shard_map/ppermute | solution.py:502
  24.4 33.5 %collective-permute-start.1 = (bf16[2,4,128,128]{3,2,1,0:T(8,128)(2,1)}, bf16[2,4,128,128]{3,2,1,0:T(8,128)(2,1)S(1)}, u32[]{:S(2)}, u32[]{:S(2)}) collective-permute-start(bf16[2,4,128,128]{3,2,1,0:T(8,128)(2,1)} %get-tuple-element.37), channel_id=1, source_target_pairs={{0,9},{1,8},{2,11},{3,10},{4,13},{5,12},{6,15},{7,14},{8,1},{9,0},... | collective-permute-start | bytes 786440 | tf_op jit(solution)/shard_map/ppermute | solution.py:502
  26.5 31.5 %collective-permute-start.2 = (bf16[2,4,128,128]{3,2,1,0:T(8,128)(2,1)}, bf16[2,4,128,128]{3,2,1,0:T(8,128)(2,1)}, u32[]{:S(2)}, u32[]{:S(2)}) collective-permute-start(bf16[2,4,128,128]{3,2,1,0:T(8,128)(2,1)} %get-tuple-element.38), channel_id=1, source_target_pairs={{0,7},{1,2},{2,1},{3,4},{4,3},{5,6},{6,5},{7,0},{8,15},{9,10},{10,... | collective-permute-start | bytes 786440 | tf_op jit(solution)/shard_map/ppermute | solution.py:502
  30.9 27.0 %collective-permute-start.3 = (bf16[2,4,128,128]{3,2,1,0:T(8,128)(2,1)}, bf16[2,4,128,128]{3,2,1,0:T(8,128)(2,1)}, u32[]{:S(2)}, u32[]{:S(2)}) collective-permute-start(bf16[2,4,128,128]{3,2,1,0:T(8,128)(2,1)} %get-tuple-element.39), channel_id=1, source_target_pairs={{0,15},{1,10},{2,9},{3,12},{4,11},{5,14},{6,13},{7,8},{8,7},{9,2},... | collective-permute-start | bytes 786440 | tf_op jit(solution)/shard_map/ppermute | solution.py:502
  34.9 10.6 %copy-start.5 = (bf16[2,2,4,128,128]{4,3,2,1,0:T(8,128)(2,1)S(1)}, bf16[2,2,4,128,128]{4,3,2,1,0:T(8,128)(2,1)}, u32[]{:S(2)}) copy-start(bf16[2,2,4,128,128]{4,3,2,1,0:T(8,128)(2,1)} %copy-done.4) | copy-start | bytes 1572868
  55.7 0.7 copy-start.6
  58.0 27.4 %copy-start.7 = (bf16[2,4,128,128]{3,2,1,0:T(8,128)(2,1)S(1)}, bf16[2,4,128,128]{3,2,1,0:T(8,128)(2,1)}, u32[]{:S(2)}) copy-start(bf16[2,4,128,128]{3,2,1,0:T(8,128)(2,1)} %copy-done.6) | copy-start | bytes 786436
  73.2 27.7 %all-to-all-start.1 = ((f32[32,16,128]{2,1,0:T(8,128)}), f32[32,16,128]{2,1,0:T(8,128)S(1)}, u32[]{:S(2)}, u32[]{:S(2)}) async-start(f32[32,16,128]{2,1,0:T(8,128)} %get-tuple-element.48), calls=%async_computation.1 | async-start | bytes 524288 | tf_op jit(solution)/shard_map/all_to_all | solution.py:522
  85.4 21.4 %collective-permute-start.5 = (bf16[2,4,128,128]{3,2,1,0:T(8,128)(2,1)S(1)}, bf16[2,4,128,128]{3,2,1,0:T(8,128)(2,1)S(1)}, u32[]{:S(2)}, u32[]{:S(2)}) collective-permute-start(bf16[2,4,128,128]{3,2,1,0:T(8,128)(2,1)S(1)} %copy-done.7), channel_id=1, source_target_pairs={{0,8},{1,9},{2,10},{3,11},{4,12},{5,13},{6,14},{7,15},{8,0},{9,1},... | collective-permute-start | bytes 786440 | tf_op jit(solution)/shard_map/ppermute | solution.py:502
  87.3 14.5 %collective-permute-start.6 = (bf16[4,128,128]{2,1,0:T(8,128)(2,1)}, bf16[4,128,128]{2,1,0:T(8,128)(2,1)S(1)}, u32[]{:S(2)}, u32[]{:S(2)}) collective-permute-start(bf16[4,128,128]{2,1,0:T(8,128)(2,1)} %get-tuple-element.52), channel_id=1, source_target_pairs={{0,1},{1,0},{2,3},{3,2},{4,5},{5,4},{6,7},{7,6},{8,9},{9,8},{10,11... | collective-permute-start | bytes 393224 | tf_op jit(solution)/shard_map/ppermute | solution.py:502
  89.3 12.6 %collective-permute-start.7 = (bf16[4,128,128]{2,1,0:T(8,128)(2,1)}, bf16[4,128,128]{2,1,0:T(8,128)(2,1)S(1)}, u32[]{:S(2)}, u32[]{:S(2)}) collective-permute-start(bf16[4,128,128]{2,1,0:T(8,128)(2,1)} %get-tuple-element.53), channel_id=1, source_target_pairs={{0,9},{1,8},{2,11},{3,10},{4,13},{5,12},{6,15},{7,14},{8,1},{9,0},... | collective-permute-start | bytes 393224 | tf_op jit(solution)/shard_map/ppermute | solution.py:502
  93.8 8.1 %collective-permute-start.8 = (bf16[4,128,128]{2,1,0:T(8,128)(2,1)S(1)}, bf16[4,128,128]{2,1,0:T(8,128)(2,1)S(1)}, u32[]{:S(2)}, u32[]{:S(2)}) collective-permute-start(bf16[4,128,128]{2,1,0:T(8,128)(2,1)S(1)} %get-tuple-element.54), channel_id=1, source_target_pairs={{0,7},{1,2},{2,1},{3,4},{4,3},{5,6},{6,5},{7,0},{8,15},{9,10},{10,... | collective-permute-start | bytes 393224 | tf_op jit(solution)/shard_map/ppermute | solution.py:502
  99.0 7.8 %collective-permute-start.9 = (bf16[4,128,128]{2,1,0:T(8,128)(2,1)S(1)}, bf16[4,128,128]{2,1,0:T(8,128)(2,1)S(1)}, u32[]{:S(2)}, u32[]{:S(2)}) collective-permute-start(bf16[4,128,128]{2,1,0:T(8,128)(2,1)S(1)} %get-tuple-element.55), channel_id=1, source_target_pairs={{0,15},{1,10},{2,9},{3,12},{4,11},{5,14},{6,13},{7,8},{8,7},{9,2},... | collective-permute-start | bytes 393224 | tf_op jit(solution)/shard_map/ppermute | solution.py:502
  106.8 4.5 %copy-start.8 = (s32[1,128]{1,0:T(1,128)S(1)}, s32[1,128]{1,0:T(1,128)}, u32[]{:S(2)}) copy-start(s32[1,128]{1,0:T(1,128)} %pos_hbm.1) | copy-start | bytes 1540
  106.8 31.8 %all-to-all-start.2 = ((bf16[16,144,256]{2,1,0:T(8,128)(2,1)}), bf16[16,144,256]{2,1,0:T(8,128)(2,1)S(1)}, u32[]{:S(2)}, u32[]{:S(2)}) async-start(bf16[16,144,256]{2,1,0:T(8,128)(2,1)} %add.63), calls=%async_computation.2 | async-start | bytes 2359296 | tf_op jit(solution)/shard_map/all_to_all | solution.py:525

commit v3 on v2

--- a/solution.py
+++ b/solution.py
@@ -176,7 +176,7 @@
             kt_ref[w, :, j * BLK : (j + 1) * BLK] = r.T.astype(bf16)
         return carry
 
-    lax.fori_loop(0, n // per, ready, 0)
+    lax.fori_loop(0, n // per, ready, 0, unroll=2)
 
 
 def prep(kv, table, ks):
@@ -200,11 +200,11 @@
     take = iter(refs)
     get = lambda count: [next(take) for _ in range(count)]
     parts = get(2 if stage == 0 else 4)
-    kv_hbm, cs_hbm, kr_hbm, kt_hbm, qs_ref = get(5)
+    kv_ref, cs_ref, kr_ref, kt_ref, qs_ref = get(5)
     dk_in, dv_in, tq_in = get(3) if stage else (None,) * 3
     grads = get(2 if stage == 0 else 4)
     last = get(3 if stage == 0 else 2)
-    s_scr, p_scr, qd_scr, kv_ref, cs_ref, kr_ref, kt_ref, q_scr, dq_scr, m_scr, e_scr, gq_scr, dk_ref, dv_ref = get(14)
+    s_scr, p_scr, qd_scr, q_scr, dq_scr, m_scr, e_scr, gq_scr, dk_ref, dv_ref = get(10)
     tq_ref, sems, kv_sems = get(3)
     n = kv_ref.shape[0]
     first, second = pl.ds(0, SUB), pl.ds(SUB, SUB)
@@ -213,7 +213,6 @@
     else:
         places = lambda r: ((r[0], 0, first), (r[2], 0, second), (r[1], 1, first), (r[3], 1, second))
     pieces = [(src, qd_scr.at[u, :, heads]) for src, u, heads in places(parts)]
-    pieces += [(kr_hbm, kr_ref), (kv_hbm, kv_ref), (cs_hbm, cs_ref), (kt_hbm, kt_ref)]
     if stage:
         pieces += [(dk_in, dk_ref), (dv_in, dv_ref)]
     copies = [pltpu.make_async_copy(src, dst, kv_sems.at[i]) for i, (src, dst) in enumerate(pieces)]
@@ -225,11 +224,16 @@
         tq_ref[...] = jnp.zeros_like(tq_ref)
     else:
         tq_ref[...] = tq_in[...]
-    rows, (kr_copy, kv_copy, cs_copy, kt_copy), sums = copies[:4], copies[4:8], copies[8:]
+    rows, sums = copies[:4], copies[4:]
     per = KEYS // BLK
 
-    def wait(u, *which):
-        @pl.when(u == 0)
+    outs = [(gq_scr.at[u, heads], dst) for dst, u, heads in places(grads)]
+    if stage == 0:
+        outs += [(dk_ref, last[0]), (dv_ref, last[1])]
+    copies = [pltpu.make_async_copy(src, dst, sems.at[i]) for i, (src, dst) in enumerate(outs)]
+
+    def wait(u, at, *which):
+        @pl.when(u == at)
         def _():
             for copy in which:
                 copy.wait()
@@ -240,7 +244,8 @@
 
     def unit(u, carry):
         b0, b1 = blocks_ref[2 * u], blocks_ref[2 * u + 1]
-        wait(u, *rows, cs_copy)
+        wait(u, 0, *rows[:2])
+        wait(u, 1, *rows[2:])
         tabs = []
         for b in (b0, b1):
             toks = pl.ds(pl.multiple_of(b * BLK, BLK), BLK)
@@ -252,8 +257,6 @@
         dq_scr[...] = jnp.zeros_like(dq_scr)
         token = jnp.where(lane < ROWS // 2, b0, b1) * BLK + (lane & (BLK - 1)) - sub8
         steps = jnp.maximum(b0, b1) // per + 1
-
-        wait(u, kr_copy, kv_copy)
 
         def look(w, stats, masked):
             m, l, d = stats
@@ -287,7 +290,7 @@
         m_scr[...] = jnp.broadcast_to(shift, m_scr.shape)
         e_scr[...] = jnp.broadcast_to(delta, e_scr.shape)
 
-        wait(u, kt_copy, *sums)
+        wait(u, 0, *sums)
 
         def back(w, carry):
             shift, delta = m_scr[...][None], e_scr[...][None]
@@ -315,15 +318,19 @@
             g = unturn(g, cos, sin)
             gq_scr[u, h] = (g * qs_ref[h : h + 1, :]).astype(bf16)
             tq_ref[h : h + 1, :] += jnp.sum(g * qd_scr[u, 0, h].astype(f32), axis=0, keepdims=True)
+        for i in range(2):
+
+            @pl.when(u == i)
+            def _():
+                for copy in copies[2 * i : 2 * i + 2]:
+                    copy.start()
+
         return carry
 
     lax.fori_loop(0, 2, unit, 0)
-    outs = [(gq_scr.at[u, heads], dst) for dst, u, heads in places(grads)]
     if stage == 0:
-        outs += [(dk_ref, last[0]), (dv_ref, last[1])]
-    copies = [pltpu.make_async_copy(src, dst, sems.at[i]) for i, (src, dst) in enumerate(outs)]
-    for copy in copies:
-        copy.start()
+        for copy in copies[4:]:
+            copy.start()
     if stage == 0:
         last[2][...] = tq_ref[...]
         for copy in copies:
@@ -363,16 +370,12 @@
     return pl.pallas_call(
         lambda *refs: attend_kernel(stage, *refs),
         out_shape=out_shape,
-        in_specs=[SMEM] + [ANY] * (len(parts) + 4) + [VMEM] + ([ANY, ANY, VMEM] if stage else []),
+        in_specs=[SMEM] + [ANY] * len(parts) + [VMEM] * 5 + ([ANY, ANY, VMEM] if stage else []),
         out_specs=out_specs,
         scratch_shapes=[
             pltpu.VMEM((length, ROWS), f32),
             pltpu.VMEM((length, ROWS), f32),
             pltpu.VMEM((2, 2, 2 * SUB, BLK, HD), bf16),
-            pltpu.VMEM(kv.shape, bf16),
-            pltpu.VMEM((length, 2 * HD), f32),
-            pltpu.VMEM((length, HD), bf16),
-            pltpu.VMEM((length // KEYS, HD, KEYS), bf16),
             pltpu.VMEM((ROWS, HD), bf16),
             pltpu.VMEM((HD, ROWS), f32),
             pltpu.VMEM((8, ROWS), f32),

time: 141 us -> 142 us (level)
  no operation moved by 1% of the time
where the time goes in v3:
time: 142 us; the launch traced here: 140 us
  starting transfers between devices  60.1 us (42%)
  waiting for transfers between devices  41.1 us (29%)
  Pallas kernels  34.8 us (25%)
  local copies, waits for them, and re-layouts  1.54 us (1%)
    ppermute x10, starting transfers between devices, send(): return lax.ppermute(a, 'seq', pairs(flip, step))  30.6 us
    all_to_all x1, waiting for transfers between devices, shards(): dkv = lax.all_to_all(dkv, 'seq', 0, 0, tiled=True)  25.5 us
    pallas_call x2, Pallas kernels, attend(): pl.pallas_call(lambda *refs: attend_kernel(stage, *refs), out_shape=out_s...  24.9 us
    all_to_all x1, starting transfers between devices, shards(): term = lax.all_to_all(term, 'dp', 0, 0, tiled=True)  12.2 us
    all_to_all x1, starting transfers between devices, shards(): lax.all_to_all(pack_kv(keys[0], values[0], positions, n), 'seq', 0, 0, ti...  12 us
    all_to_all x1, waiting for transfers between devices, shards(): lax.all_to_all(pack_kv(keys[0], values[0], positions, n), 'seq', 0, 0, ti...  8.22 us
    ppermute x10, waiting for transfers between devices, send(): return lax.ppermute(a, 'seq', pairs(flip, step))  7.35 us
    all_to_all x1, starting transfers between devices, shards(): dkv = lax.all_to_all(dkv, 'seq', 0, 0, tiled=True)  5.32 us
  transfers between devices with their start and end apart: 13, of which 4 were waited for; matrix products, arithmetic and copies ran while one was open for 1% of the time, Pallas kernels for 12%

profile of v3, /device:TPU:1, one launch (start us, length us, event | category | flops | bytes accessed | tf_op | source)
XLA Modules:
  0.0 139.9 jit_solution(4004284777689228856)
XLA Ops:
  0.6 2.2 %pack_kv.1 = bf16[16,144,256]{2,1,0:T(8,128)(2,1)} custom-call(bf16[128,512]{1,0:T(8,128)(2,1)} %bitcast.36, bf16[128,512]{1,0:T(8,128)(2,1)} %bitcast.37, s32[1,128]{1,0:T(1,128)} %pos_hbm.1), custom_call_target="tpu_custom_call" | custom-call | bytes 2097152 | tf_op jit(solution)/shard_map/pack_kv/pallas_call | solution.py:99
  2.8 12.0 %all-to-all-start = ((bf16[16,144,256]{2,1,0:T(8,128)(2,1)}), bf16[16,144,256]{2,1,0:T(8,128)(2,1)S(1)}, u32[]{:S(2)}, u32[]{:S(2)}) async-start(bf16[16,144,256]{2,1,0:T(8,128)(2,1)} %pack_kv.1), calls=%async_computation | async-start | bytes 2359296 | tf_op jit(solution)/shard_map/all_to_all | solution.py:507
  15.0 2.3 %pack.1 = (bf16[2,2,4,128,128]{4,3,2,1,0:T(8,128)(2,1)S(1)}, bf16[2,2,4,128,128]{4,3,2,1,0:T(8,128)(2,1)}, bf16[2,4,128,128]{3,2,1,0:T(8,128)(2,1)}, bf16[2,4,12...) custom-call(s32[2]{0:T(128)S(1)} %pad_add_fusion.place_ref, ...), custom_call_target="tpu_custom_call" | custom-call | bytes 4194304 | tf_op jit(solution)/shard_map/pack/pallas_call | solution.py:138
  18.1 3.3 %collective-permute-start.4 = (bf16[2,2,4,128,128]{4,3,2,1,0:T(8,128)(2,1)}, bf16[2,2,4,128,128]{4,3,2,1,0:T(8,128)(2,1)S(1)}, u32[]{:S(2)}, u32[]{:S(2)}) collective-permute-start(bf16[2,2,4,128,128]{4,3,2,1,0:T(8,128)(2,1)} %get-tuple-element.44), channel_id=1, source_target_pairs={{0,8},{1,9},{2,10},{3,11},{4,12},{5,13},{6,14},{7,15},{8,0},{9,1},... | collective-permute-start | bytes 1572872 | tf_op jit(solution)/shard_map/ppermute | solution.py:505
  21.3 3.1 %collective-permute-start = (bf16[2,4,128,128]{3,2,1,0:T(8,128)(2,1)}, bf16[2,4,128,128]{3,2,1,0:T(8,128)(2,1)S(1)}, u32[]{:S(2)}, u32[]{:S(2)}) collective-permute-start(bf16[2,4,128,128]{3,2,1,0:T(8,128)(2,1)} %get-tuple-element.36), channel_id=1, source_target_pairs={{0,1},{1,0},{2,3},{3,2},{4,5},{5,4},{6,7},{7,6},{8,9},{9,8},{10,11... | collective-permute-start | bytes 786440 | tf_op jit(solution)/shard_map/ppermute | solution.py:505
  24.4 2.0 %collective-permute-start.1 = (bf16[2,4,128,128]{3,2,1,0:T(8,128)(2,1)}, bf16[2,4,128,128]{3,2,1,0:T(8,128)(2,1)S(1)}, u32[]{:S(2)}, u32[]{:S(2)}) collective-permute-start(bf16[2,4,128,128]{3,2,1,0:T(8,128)(2,1)} %get-tuple-element.37), channel_id=1, source_target_pairs={{0,9},{1,8},{2,11},{3,10},{4,13},{5,12},{6,15},{7,14},{8,1},{9,0},... | collective-permute-start | bytes 786440 | tf_op jit(solution)/shard_map/ppermute | solution.py:505
  26.5 4.5 %collective-permute-start.2 = (bf16[2,4,128,128]{3,2,1,0:T(8,128)(2,1)}, bf16[2,4,128,128]{3,2,1,0:T(8,128)(2,1)}, u32[]{:S(2)}, u32[]{:S(2)}) collective-permute-start(bf16[2,4,128,128]{3,2,1,0:T(8,128)(2,1)} %get-tuple-element.38), channel_id=1, source_target_pairs={{0,7},{1,2},{2,1},{3,4},{4,3},{5,6},{6,5},{7,0},{8,15},{9,10},{10,... | collective-permute-start | bytes 786440 | tf_op jit(solution)/shard_map/ppermute | solution.py:505
  30.9 3.1 %collective-permute-start.3 = (bf16[2,4,128,128]{3,2,1,0:T(8,128)(2,1)}, bf16[2,4,128,128]{3,2,1,0:T(8,128)(2,1)}, u32[]{:S(2)}, u32[]{:S(2)}) collective-permute-start(bf16[2,4,128,128]{3,2,1,0:T(8,128)(2,1)} %get-tuple-element.39), channel_id=1, source_target_pairs={{0,15},{1,10},{2,9},{3,12},{4,11},{5,14},{6,13},{7,8},{8,7},{9,2},... | collective-permute-start | bytes 786440 | tf_op jit(solution)/shard_map/ppermute | solution.py:505
  35.0 8.2 %all-to-all-done.kv_ref.refs_3_.refs_5_ = bf16[16,144,256]{2,1,0:T(8,128)(2,1)S(1)} async-done(((bf16[16,144,256]{2,1,0:T(8,128)(2,1)}), bf16[16,144,256]{2,1,0:T(8,128)(2,1)S(1)}, u32[]{:S(2)}, u32[]{:S(2)}) %all-to-all-start) | async-done | bytes 1179680 | tf_op jit(solution)/shard_map/all_to_all | solution.py:507
  43.2 1.9 %prep.1 = (f32[2048,256]{1,0:T(8,128)S(1)}, bf16[2048,128]{1,0:T(8,128)(2,1)S(1)}, bf16[4,128,512]{2,1,0:T(8,128)(2,1)S(1)}) custom-call(bf16[16,144,256]{2,1,0:T(8,128)(2,1)S(1)} %all-to-all-done.kv_ref.refs_3_.refs_5_, bf16[2,128,512]{2,1,0:T(8,128)(2,1)S(1)} %maximum_maximum_fusion.table_ref, f32[1,128]{1,0:T(1,128)S(1)} %constant_dynamic-slice_fusion.ks_ref), custom_call_target="tpu_custom_call" | custom-call | flops 536870912 | bytes 5242880 | tf_op jit(solution)/shard_map/prep/pallas_call | solution.py:184
  45.1 9.7 %attend.2 = (bf16[2,4,128,128]{3,2,1,0:T(8,128)(2,1)S(1)}, bf16[2,4,128,128]{3,2,1,0:T(8,128)(2,1)S(1)}, f32[2048,128]{1,0:T(8,128)S(1)}, f32[2048,128]{1,0:T(8,128)S(1)}, f32[8,128]{1,0:T(8,128)S(1)}) custom-call(s32[4]{0:T(128)S(1)} %pad_add_fusion.2.refs_0_, bf16[2,2,4,128,128]{4,3,2,1,0:T(8,128)(2,1)S(1)} %copy-done.5, ...), custom_call_target="tpu_custom_call" | custom-call | flops 5368709120 | bytes 8388608 | tf_op jit(solution)/shard_map/attend/pallas_call | solution.py:370
  55.6 2.3 %collective-permute-done.1.refs_2_ = bf16[2,4,128,128]{3,2,1,0:T(8,128)(2,1)S(1)} collective-permute-done((bf16[2,4,128,128]{3,2,1,0:T(8,128)(2,1)}, bf16[2,4,128,128]{3,2,1,0:T(8,128)(2,1)S(1)}, u32[]{:S(2)}, u32[]{:S(2)}) %collective-permute-start.1) | collective-permute-done | bytes 262176 | tf_op jit(solution)/shard_map/ppermute | solution.py:505
  58.0 15.2 %attend.3 = (bf16[4,128,128]{2,1,0:T(8,128)(2,1)}, bf16[4,128,128]{2,1,0:T(8,128)(2,1)}, bf16[4,128,128]{2,1,0:T(8,128)(2,1)S(1)}, bf16[4,128,128]{2,1,0:T(8,128...) custom-call(s32[4]{0:T(128)S(1)} %pad_add_fusion.1.refs_0_, ...), custom_call_target="tpu_custom_call" | custom-call | flops 5368709120 | bytes 8388608 | tf_op jit(solution)/shard_map/attend/pallas_call | solution.py:370
  73.2 12.2 %all-to-all-start.1 = ((f32[32,16,128]{2,1,0:T(8,128)}), f32[32,16,128]{2,1,0:T(8,128)S(1)}, u32[]{:S(2)}, u32[]{:S(2)}) async-start(f32[32,16,128]{2,1,0:T(8,128)} %get-tuple-element.48), calls=%async_computation.1 | async-start | bytes 524288 | tf_op jit(solution)/shard_map/all_to_all | solution.py:525
  85.3 1.9 %collective-permute-start.5 = (bf16[2,4,128,128]{3,2,1,0:T(8,128)(2,1)S(1)}, bf16[2,4,128,128]{3,2,1,0:T(8,128)(2,1)S(1)}, u32[]{:S(2)}, u32[]{:S(2)}) collective-permute-start(bf16[2,4,128,128]{3,2,1,0:T(8,128)(2,1)S(1)} %copy-done.7), channel_id=1, source_target_pairs={{0,8},{1,9},{2,10},{3,11},{4,12},{5,13},{6,14},{7,15},{8,0},{9,1},... | collective-permute-start | bytes 786440 | tf_op jit(solution)/shard_map/ppermute | solution.py:505
  87.3 1.9 %collective-permute-start.6 = (bf16[4,128,128]{2,1,0:T(8,128)(2,1)}, bf16[4,128,128]{2,1,0:T(8,128)(2,1)S(1)}, u32[]{:S(2)}, u32[]{:S(2)}) collective-permute-start(bf16[4,128,128]{2,1,0:T(8,128)(2,1)} %get-tuple-element.52), channel_id=1, source_target_pairs={{0,1},{1,0},{2,3},{3,2},{4,5},{5,4},{6,7},{7,6},{8,9},{9,8},{10,11... | collective-permute-start | bytes 393224 | tf_op jit(solution)/shard_map/ppermute | solution.py:505
  89.2 4.5 %collective-permute-start.7 = (bf16[4,128,128]{2,1,0:T(8,128)(2,1)}, bf16[4,128,128]{2,1,0:T(8,128)(2,1)S(1)}, u32[]{:S(2)}, u32[]{:S(2)}) collective-permute-start(bf16[4,128,128]{2,1,0:T(8,128)(2,1)} %get-tuple-element.53), channel_id=1, source_target_pairs={{0,9},{1,8},{2,11},{3,10},{4,13},{5,12},{6,15},{7,14},{8,1},{9,0},... | collective-permute-start | bytes 393224 | tf_op jit(solution)/shard_map/ppermute | solution.py:505
  93.7 4.4 %collective-permute-start.8 = (bf16[4,128,128]{2,1,0:T(8,128)(2,1)S(1)}, bf16[4,128,128]{2,1,0:T(8,128)(2,1)S(1)}, u32[]{:S(2)}, u32[]{:S(2)}) collective-permute-start(bf16[4,128,128]{2,1,0:T(8,128)(2,1)S(1)} %get-tuple-element.54), channel_id=1, source_target_pairs={{0,7},{1,2},{2,1},{3,4},{4,3},{5,6},{6,5},{7,0},{8,15},{9,10},{10,... | collective-permute-start | bytes 393224 | tf_op jit(solution)/shard_map/ppermute | solution.py:505
  98.1 1.9 %collective-permute-start.9 = (bf16[4,128,128]{2,1,0:T(8,128)(2,1)S(1)}, bf16[4,128,128]{2,1,0:T(8,128)(2,1)S(1)}, u32[]{:S(2)}, u32[]{:S(2)}) collective-permute-start(bf16[4,128,128]{2,1,0:T(8,128)(2,1)S(1)} %get-tuple-element.55), channel_id=1, source_target_pairs={{0,15},{1,10},{2,9},{3,12},{4,11},{5,14},{6,13},{7,8},{8,7},{9,2},... | collective-permute-start | bytes 393224 | tf_op jit(solution)/shard_map/ppermute | solution.py:505
  101.0 5.0 %collective-permute-done.9.db_ref = bf16[4,128,128]{2,1,0:T(8,128)(2,1)S(1)} collective-permute-done((bf16[4,128,128]{2,1,0:T(8,128)(2,1)S(1)}, bf16[4,128,128]{2,1,0:T(8,128)(2,1)S(1)}, u32[]{:S(2)}, u32[]{:S(2)}) %collective-permute-start.9) | collective-permute-done | bytes 131104 | tf_op jit(solution)/shard_map/ppermute | solution.py:505
  105.9 5.3 %all-to-all-start.2 = ((bf16[16,144,256]{2,1,0:T(8,128)(2,1)}), bf16[16,144,256]{2,1,0:T(8,128)(2,1)S(1)}, u32[]{:S(2)}, u32[]{:S(2)}) async-start(bf16[16,144,256]{2,1,0:T(8,128)(2,1)} %add.63), calls=%async_computation.2 | async-start | bytes 2359296 | tf_op jit(solution)/shard_map/all_to_all | solution.py:528
  111.7 1.8 %unpack.1 = bf16[128,4096]{1,0:T(8,128)(2,1)} custom-call(s32[2]{0:T(128)S(1)} %pad_add_fusion.place_ref, bf16[2,4,128,128]{3,2,1,0:T(8,128)(2,1)S(1)} %get-tuple-element.56.own_ref, bf16[2,4,128,128]{3,2,1,0:T(8,128)(2,1)S(1)} %collective-permute-done.5.x_ref, bf16[4,128,128]{2,1,0:T(8,128)(2,1)S(1)} %collective-permute-done.6.za_ref, ...), custom_call_target="tpu_custom_call" | custom-call | bytes 2097152 | tf_op jit(solution)/shard_map/unpack/pallas_call | solution.py:442
  113.5 25.5 %all-to-all-done.2.dkv_ref = bf16[16,144,256]{2,1,0:T(8,128)(2,1)S(1)} async-done(((bf16[16,144,256]{2,1,0:T(8,128)(2,1)}), bf16[16,144,256]{2,1,0:T(8,128)(2,1)S(1)}, u32[]{:S(2)}, u32[]{:S(2)}) %all-to-all-start.2) | async-done | bytes 1179680 | tf_op jit(solution)/shard_map/all_to_all | solution.py:528
  139.0 0.9 final.1
  (42 shorter events, 3.8 us)
Async XLA Ops:
  0.6 33.7 %copy-start = (f32[4096]{0:T(1024)S(1)}, f32[4096]{0:T(1024)}, u32[]{:S(2)}) copy-start(f32[4096]{0:T(1024)} %param.12) | copy-start | bytes 49156
  2.8 12.2 %copy-start.1 = (bf16[1,128,4096]{2,1,0:T(8,128)(2,1)S(1)}, bf16[1,128,4096]{2,1,0:T(8,128)(2,1)}, u32[]{:S(2)}) copy-start(bf16[1,128,4096]{2,1,0:T(8,128)(2,1)} %param.7) | copy-start | bytes 3145732
  2.8 12.2 %copy-start.2 = (bf16[1,128,4096]{2,1,0:T(8,128)(2,1)S(1)}, bf16[1,128,4096]{2,1,0:T(8,128)(2,1)}, u32[]{:S(2)}) copy-start(bf16[1,128,4096]{2,1,0:T(8,128)(2,1)} %param.10) | copy-start | bytes 3145732
  2.8 40.4 %all-to-all-start = ((bf16[16,144,256]{2,1,0:T(8,128)(2,1)}), bf16[16,144,256]{2,1,0:T(8,128)(2,1)S(1)}, u32[]{:S(2)}, u32[]{:S(2)}) async-start(bf16[16,144,256]{2,1,0:T(8,128)(2,1)} %pack_kv.1), calls=%async_computation | async-start | bytes 2359296 | tf_op jit(solution)/shard_map/all_to_all | solution.py:507
  14.9 19.4 %copy-start.3 = (f32[512]{0:T(512)S(1)}, f32[512]{0:T(512)}, u32[]{:S(2)}) copy-start(f32[512]{0:T(512)} %param.13) | copy-start | bytes 6148
  17.3 0.8 copy-start.4
  18.1 27.0 %collective-permute-start.4 = (bf16[2,2,4,128,128]{4,3,2,1,0:T(8,128)(2,1)}, bf16[2,2,4,128,128]{4,3,2,1,0:T(8,128)(2,1)S(1)}, u32[]{:S(2)}, u32[]{:S(2)}) collective-permute-start(bf16[2,2,4,128,128]{4,3,2,1,0:T(8,128)(2,1)} %get-tuple-element.44), channel_id=1, source_target_pairs={{0,8},{1,9},{2,10},{3,11},{4,12},{5,13},{6,14},{7,15},{8,0},{9,1},... | collective-permute-start | bytes 1572872 | tf_op jit(solution)/shard_map/ppermute | solution.py:505
  21.3 34.3 %collective-permute-start = (bf16[2,4,128,128]{3,2,1,0:T(8,128)(2,1)}, bf16[2,4,128,128]{3,2,1,0:T(8,128)(2,1)S(1)}, u32[]{:S(2)}, u32[]{:S(2)}) collective-permute-start(bf16[2,4,128,128]{3,2,1,0:T(8,128)(2,1)} %get-tuple-element.36), channel_id=1, source_target_pairs={{0,1},{1,0},{2,3},{3,2},{4,5},{5,4},{6,7},{7,6},{8,9},{9,8},{10,11... | collective-permute-start | bytes 786440 | tf_op jit(solution)/shard_map/ppermute | solution.py:505
  24.4 33.5 %collective-permute-start.1 = (bf16[2,4,128,128]{3,2,1,0:T(8,128)(2,1)}, bf16[2,4,128,128]{3,2,1,0:T(8,128)(2,1)S(1)}, u32[]{:S(2)}, u32[]{:S(2)}) collective-permute-start(bf16[2,4,128,128]{3,2,1,0:T(8,128)(2,1)} %get-tuple-element.37), channel_id=1, source_target_pairs={{0,9},{1,8},{2,11},{3,10},{4,13},{5,12},{6,15},{7,14},{8,1},{9,0},... | collective-permute-start | bytes 786440 | tf_op jit(solution)/shard_map/ppermute | solution.py:505
  26.5 31.5 %collective-permute-start.2 = (bf16[2,4,128,128]{3,2,1,0:T(8,128)(2,1)}, bf16[2,4,128,128]{3,2,1,0:T(8,128)(2,1)}, u32[]{:S(2)}, u32[]{:S(2)}) collective-permute-start(bf16[2,4,128,128]{3,2,1,0:T(8,128)(2,1)} %get-tuple-element.38), channel_id=1, source_target_pairs={{0,7},{1,2},{2,1},{3,4},{4,3},{5,6},{6,5},{7,0},{8,15},{9,10},{10,... | collective-permute-start | bytes 786440 | tf_op jit(solution)/shard_map/ppermute | solution.py:505
  30.9 27.0 %collective-permute-start.3 = (bf16[2,4,128,128]{3,2,1,0:T(8,128)(2,1)}, bf16[2,4,128,128]{3,2,1,0:T(8,128)(2,1)}, u32[]{:S(2)}, u32[]{:S(2)}) collective-permute-start(bf16[2,4,128,128]{3,2,1,0:T(8,128)(2,1)} %get-tuple-element.39), channel_id=1, source_target_pairs={{0,15},{1,10},{2,9},{3,12},{4,11},{5,14},{6,13},{7,8},{8,7},{9,2},... | collective-permute-start | bytes 786440 | tf_op jit(solution)/shard_map/ppermute | solution.py:505
  34.9 10.2 %copy-start.5 = (bf16[2,2,4,128,128]{4,3,2,1,0:T(8,128)(2,1)S(1)}, bf16[2,2,4,128,128]{4,3,2,1,0:T(8,128)(2,1)}, u32[]{:S(2)}) copy-start(bf16[2,2,4,128,128]{4,3,2,1,0:T(8,128)(2,1)} %copy-done.4) | copy-start | bytes 1572868
  54.9 0.7 copy-start.6
  58.0 27.4 %copy-start.7 = (bf16[2,4,128,128]{3,2,1,0:T(8,128)(2,1)S(1)}, bf16[2,4,128,128]{3,2,1,0:T(8,128)(2,1)}, u32[]{:S(2)}) copy-start(bf16[2,4,128,128]{3,2,1,0:T(8,128)(2,1)} %copy-done.6) | copy-start | bytes 786436
  73.2 26.9 %all-to-all-start.1 = ((f32[32,16,128]{2,1,0:T(8,128)}), f32[32,16,128]{2,1,0:T(8,128)S(1)}, u32[]{:S(2)}, u32[]{:S(2)}) async-start(f32[32,16,128]{2,1,0:T(8,128)} %get-tuple-element.48), calls=%async_computation.1 | async-start | bytes 524288 | tf_op jit(solution)/shard_map/all_to_all | solution.py:525
  85.3 20.6 %collective-permute-start.5 = (bf16[2,4,128,128]{3,2,1,0:T(8,128)(2,1)S(1)}, bf16[2,4,128,128]{3,2,1,0:T(8,128)(2,1)S(1)}, u32[]{:S(2)}, u32[]{:S(2)}) collective-permute-start(bf16[2,4,128,128]{3,2,1,0:T(8,128)(2,1)S(1)} %copy-done.7), channel_id=1, source_target_pairs={{0,8},{1,9},{2,10},{3,11},{4,12},{5,13},{6,14},{7,15},{8,0},{9,1},... | collective-permute-start | bytes 786440 | tf_op jit(solution)/shard_map/ppermute | solution.py:505
  87.3 13.7 %collective-permute-start.6 = (bf16[4,128,128]{2,1,0:T(8,128)(2,1)}, bf16[4,128,128]{2,1,0:T(8,128)(2,1)S(1)}, u32[]{:S(2)}, u32[]{:S(2)}) collective-permute-start(bf16[4,128,128]{2,1,0:T(8,128)(2,1)} %get-tuple-element.52), channel_id=1, source_target_pairs={{0,1},{1,0},{2,3},{3,2},{4,5},{5,4},{6,7},{7,6},{8,9},{9,8},{10,11... | collective-permute-start | bytes 393224 | tf_op jit(solution)/shard_map/ppermute | solution.py:505
  89.2 11.7 %collective-permute-start.7 = (bf16[4,128,128]{2,1,0:T(8,128)(2,1)}, bf16[4,128,128]{2,1,0:T(8,128)(2,1)S(1)}, u32[]{:S(2)}, u32[]{:S(2)}) collective-permute-start(bf16[4,128,128]{2,1,0:T(8,128)(2,1)} %get-tuple-element.53), channel_id=1, source_target_pairs={{0,9},{1,8},{2,11},{3,10},{4,13},{5,12},{6,15},{7,14},{8,1},{9,0},... | collective-permute-start | bytes 393224 | tf_op jit(solution)/shard_map/ppermute | solution.py:505
  93.7 7.2 %collective-permute-start.8 = (bf16[4,128,128]{2,1,0:T(8,128)(2,1)S(1)}, bf16[4,128,128]{2,1,0:T(8,128)(2,1)S(1)}, u32[]{:S(2)}, u32[]{:S(2)}) collective-permute-start(bf16[4,128,128]{2,1,0:T(8,128)(2,1)S(1)} %get-tuple-element.54), channel_id=1, source_target_pairs={{0,7},{1,2},{2,1},{3,4},{4,3},{5,6},{6,5},{7,0},{8,15},{9,10},{10,... | collective-permute-start | bytes 393224 | tf_op jit(solution)/shard_map/ppermute | solution.py:505
  98.1 7.8 %collective-permute-start.9 = (bf16[4,128,128]{2,1,0:T(8,128)(2,1)S(1)}, bf16[4,128,128]{2,1,0:T(8,128)(2,1)S(1)}, u32[]{:S(2)}, u32[]{:S(2)}) collective-permute-start(bf16[4,128,128]{2,1,0:T(8,128)(2,1)S(1)} %get-tuple-element.55), channel_id=1, source_target_pairs={{0,15},{1,10},{2,9},{3,12},{4,11},{5,14},{6,13},{7,8},{8,7},{9,2},... | collective-permute-start | bytes 393224 | tf_op jit(solution)/shard_map/ppermute | solution.py:505
  105.9 5.3 %copy-start.8 = (s32[1,128]{1,0:T(1,128)S(1)}, s32[1,128]{1,0:T(1,128)}, u32[]{:S(2)}) copy-start(s32[1,128]{1,0:T(1,128)} %pos_hbm.1) | copy-start | bytes 1540
  105.9 33.1 %all-to-all-start.2 = ((bf16[16,144,256]{2,1,0:T(8,128)(2,1)}), bf16[16,144,256]{2,1,0:T(8,128)(2,1)S(1)}, u32[]{:S(2)}, u32[]{:S(2)}) async-start(bf16[16,144,256]{2,1,0:T(8,128)(2,1)} %add.63), calls=%async_computation.2 | async-start | bytes 2359296 | tf_op jit(solution)/shard_map/all_to_all | solution.py:528
